TPU v7x, 32 devices: a whole 2x2x4 slice. The times are simulated.
32 devices in a mesh: dp: 16 (over z, y, x), tensor: 2 (over core).
Axes of the slice: x: 2, y: 2, z: 4, core: 2. Of those that a mesh axis runs over, the one named last changes fastest.
Arguments:
- frames: bfloat16 [2, 16, 512, 768], P(None, 'dp', 'tensor'), may hold values from -6 to 6
- cotangent: bfloat16 [2, 16, 512, 768], P(None, 'dp', 'tensor'), may hold values from -6 to 6
- lengths: int32 [2, 16], P(None, 'dp'), may hold values from 102 to 512, as said below
- attn_w: float32 [4, 768, 768], P(None, 'dp', 'tensor')
- attn_m: float32 [4, 768, 768], P(None, 'dp', 'tensor'), may hold values from -6.1035156e-05 to 6.1035156e-05
- attn_v: float32 [4, 768, 768], P(None, 'dp', 'tensor'), may hold values from 7.055068e-13 to 1.12881085e-11
- ffn_w: float32 [2, 768, 3072], P(None, 'dp', 'tensor')
- ffn_m: float32 [2, 768, 3072], P(None, 'dp', 'tensor'), may hold values from -6.1035156e-05 to 6.1035156e-05
- ffn_v: float32 [2, 768, 3072], P(None, 'dp', 'tensor'), may hold values from 7.055068e-13 to 1.12881085e-11
- small_w: float32 [9216], replicated
- small_m: float32 [9216], replicated, may hold values from -0.00018310547 to 0.00018310547
- small_v: float32 [9216], replicated, may hold values from 6.349561e-12 to 1.0159298e-10
Outputs:
- output: bfloat16 [2, 16, 512, 768], P(None, 'dp', 'tensor')
- frames_grad: float32 [2, 16, 512, 768], P(None, 'dp', 'tensor')
- grad_norm: float32 [], replicated
- attn_new: float32 [4, 768, 768], P(None, 'dp', 'tensor')
- attn_m_new: float32 [4, 768, 768], P(None, 'dp', 'tensor')
- attn_v_new: float32 [4, 768, 768], P(None, 'dp', 'tensor')
- ffn_new: float32 [2, 768, 3072], P(None, 'dp', 'tensor')
- ffn_m_new: float32 [2, 768, 3072], P(None, 'dp', 'tensor')
- ffn_v_new: float32 [2, 768, 3072], P(None, 'dp', 'tensor')
- small_new: float32 [9216], replicated
- small_m_new: float32 [9216], replicated
- small_v_new: float32 [9216], replicated
Inputs may be any that keep to these rules, and one draw needn't show every extreme that they name: lengths[m, b] is the number of valid frames of utterance b of micro-batch m; some utterance has 512 valid frames.
All inputs are finite; a program needn't handle non-finite values.
Results may differ from a plain program's by a relative error of at most 0.018.
Values may be sent and summed in bfloat16 or wider, within the bound.
No kernel may reach another device: no remote copies, remote signals or barrier semaphores. Data moves between devices by JAX's collectives and lax.ppermute only.
A program may use at most 128 MiB of HBM per device.

v0:
```python
import jax
import jax.numpy as jnp
from jax import lax
from jax.sharding import PartitionSpec as P

HD = 64
D = 768
FF = 3072
SEQ = 512
STEP = 10
SMALL = 9216


EPS_NORM = 1e-05
MASK_FILL = -1e30
BETA_ONE = 0.9
BETA_TWO = 0.999
ADAM_EPS = 1e-08
CLIP_NORM = 0.1
RATE = 0.1
SMALL_RATE = 1.5
DECAY = 0.01


def matmul(left, right):
    return jnp.dot(left, right, preferred_element_type=jnp.float32)


def contract(left, right, left_dim, right_dim):
    return lax.dot_general(
        left, right, (((left_dim,), (right_dim,)), ((), ())), preferred_element_type=jnp.float32
    )


def layer_norm(values, gain, shift):
    centred = values - jnp.mean(values, -1, keepdims=True)
    spread = jnp.mean(centred * centred, -1, keepdims=True)
    return centred * lax.rsqrt(spread + EPS_NORM) * gain + shift


def exact_gelu(values):
    return jax.nn.gelu(values, approximate=False)


def adamw(weight, moment_one, moment_two, grad, rate, decay):
    new_one = BETA_ONE * moment_one + (1.0 - BETA_ONE) * grad
    new_two = BETA_TWO * moment_two + (1.0 - BETA_TWO) * grad * grad
    fixed_one = new_one / (1.0 - BETA_ONE**STEP)
    fixed_two = new_two / (1.0 - BETA_TWO**STEP)
    update = fixed_one / (jnp.sqrt(fixed_two) + ADAM_EPS) + decay * weight
    return (weight - rate * update, new_one, new_two)


def place(piece, start):
    return lax.dynamic_update_slice(jnp.zeros((SMALL,), jnp.float32), piece, (start,))


def per_device(
    frames,
    cotangent,
    lengths,
    attn_w,
    attn_m,
    attn_v,
    ffn_w,
    ffn_m,
    ffn_v,
    small_w,
    small_m,
    small_v,
):
    tensor_index = lax.axis_index("tensor")
    half = frames.shape[2]
    seq_len = half * lax.axis_size("tensor")
    width = attn_w.shape[2]
    ff_width = ffn_w.shape[2]
    heads = width // HD
    scale = HD ** (-0.5)
    blocks = seq_len // seq_len
    bias_q = lax.dynamic_slice_in_dim(small_w, tensor_index * width, width)
    bias_v = lax.dynamic_slice_in_dim(small_w, D + tensor_index * width, width)
    bias_o = small_w[2 * D : 3 * D]
    bias_two = small_w[3 * D : 4 * D]
    gain_one = small_w[4 * D : 5 * D]
    shift_one = small_w[5 * D : 6 * D]
    gain_two = small_w[6 * D : 7 * D]
    shift_two = small_w[7 * D : 8 * D]
    bias_one = lax.dynamic_slice_in_dim(small_w, 8 * D + tensor_index * ff_width, ff_width)
    key_pos = jnp.arange(seq_len)
    local_pos = tensor_index * half + jnp.arange(half)
    attn_shard = jnp.zeros(attn_w.shape, jnp.float32)
    ffn_shard = jnp.zeros(ffn_w.shape, jnp.float32)
    small_total = jnp.zeros((SMALL,), jnp.float32)
    output_rows = []
    grad_rows_all = []
    for batch_step in range(frames.shape[0]):
        current = (
            lax.all_gather(attn_w.astype(jnp.bfloat16), "dp", axis=1, tiled=True),
            lax.all_gather(ffn_w.astype(jnp.bfloat16), "dp", axis=1, tiled=True),
        )
        frame_rows = frames[batch_step, 0]
        length = lengths[batch_step, 0]
        attn_full = current[0]
        ffn_full = current[1]
        key_valid = key_pos < length
        row_valid = (local_pos < length).astype(jnp.float32)
        frames_all = lax.all_gather(frame_rows, "tensor", axis=0, tiled=True)
        query = (
            (matmul(frames_all, attn_full[0]) + bias_q)
            .astype(jnp.bfloat16)
            .reshape(seq_len, heads, HD)
        )
        keys = matmul(frames_all, attn_full[1]).astype(jnp.bfloat16).reshape(seq_len, heads, HD)
        values = (
            (matmul(frames_all, attn_full[2]) + bias_v)
            .astype(jnp.bfloat16)
            .reshape(seq_len, heads, HD)
        )
        query_blocks = query.reshape(blocks, seq_len, heads, HD)

        def scores_of(query_rows):
            scores = (
                jnp.einsum("qhd,khd->hqk", query_rows, keys, preferred_element_type=jnp.float32)
                * scale
            )
            return jnp.where(key_valid[None, None, :], scores, MASK_FILL)

        def attend(query_rows):
            scores = scores_of(query_rows)
            top = jnp.max(scores, -1, keepdims=True)
            powers = jnp.exp(scores - top)
            total = jnp.sum(powers, -1, keepdims=True)
            probs = (powers / total).astype(jnp.bfloat16)
            mixed_rows = jnp.einsum(
                "hqk,khd->qhd", probs, values, preferred_element_type=jnp.float32
            )
            return (mixed_rows.astype(jnp.bfloat16), (top + jnp.log(total))[..., 0])

        mixed_blocks, log_totals = lax.map(attend, query_blocks)
        mixed = mixed_blocks.reshape(seq_len, width)
        attended = (
            lax.psum_scatter(
                contract(mixed, attn_full[3], 1, 1), "tensor", scatter_dimension=0, tiled=True
            )
            + bias_o
        )
        hidden, norm_one_back = jax.vjp(
            layer_norm, frame_rows.astype(jnp.float32) + attended, gain_one, shift_one
        )
        hidden_all = lax.all_gather(hidden.astype(jnp.bfloat16), "tensor", axis=0, tiled=True)
        acted, gelu_back = jax.vjp(exact_gelu, matmul(hidden_all, ffn_full[0]) + bias_one)
        acted = acted.astype(jnp.bfloat16)
        outer = (
            lax.psum_scatter(
                contract(acted, ffn_full[1], 1, 1).astype(jnp.bfloat16),
                "tensor",
                scatter_dimension=0,
                tiled=True,
            ).astype(jnp.float32)
            + bias_two
        )
        result, norm_two_back = jax.vjp(layer_norm, hidden + outer, gain_two, shift_two)
        out_grad = cotangent[batch_step, 0].astype(jnp.float32) * row_valid[:, None]
        grad_two, grad_gain_two, grad_shift_two = norm_two_back(out_grad)
        grad_out_all = lax.all_gather(grad_two.astype(jnp.bfloat16), "tensor", axis=0, tiled=True)
        inner_grad = gelu_back(matmul(grad_out_all, ffn_full[1]))[0]
        inner_low = inner_grad.astype(jnp.bfloat16)
        grad_up = contract(hidden_all, inner_low, 0, 0)
        grad_down = contract(grad_out_all, acted, 0, 0)
        hidden_grad = grad_two + lax.psum_scatter(
            contract(inner_low, ffn_full[0], 1, 1).astype(jnp.bfloat16),
            "tensor",
            scatter_dimension=0,
            tiled=True,
        ).astype(jnp.float32)
        grad_one, grad_gain_one, grad_shift_one = norm_one_back(hidden_grad)
        grad_att_all = lax.all_gather(grad_one.astype(jnp.bfloat16), "tensor", axis=0, tiled=True)
        grad_proj = contract(grad_att_all, mixed, 0, 0)
        mixed_grad = (
            matmul(grad_att_all, attn_full[3])
            .astype(jnp.bfloat16)
            .reshape(blocks, seq_len, heads, HD)
        )

        def back_block(carry, item):
            query_rows, grad_rows, log_rows = item
            probs = jnp.exp(scores_of(query_rows) - log_rows[..., None])
            prob_grad = jnp.einsum(
                "qhd,khd->hqk", grad_rows, values, preferred_element_type=jnp.float32
            )
            score_grad = (
                probs * (prob_grad - jnp.sum(probs * prob_grad, -1, keepdims=True))
            ).astype(jnp.bfloat16)
            query_grad = (
                jnp.einsum("hqk,khd->qhd", score_grad, keys, preferred_element_type=jnp.float32)
                * scale
            )
            key_acc = (
                carry[0]
                + jnp.einsum(
                    "hqk,qhd->khd", score_grad, query_rows, preferred_element_type=jnp.float32
                )
                * scale
            )
            value_acc = carry[1] + jnp.einsum(
                "hqk,qhd->khd",
                probs.astype(jnp.bfloat16),
                grad_rows,
                preferred_element_type=jnp.float32,
            )
            return ((key_acc, value_acc), query_grad.astype(jnp.bfloat16))

        empty = jnp.zeros((seq_len, heads, HD), jnp.float32)
        accums, query_grads = lax.scan(
            back_block, (empty, empty), (query_blocks, mixed_grad, log_totals)
        )
        grad_query = query_grads.reshape(seq_len, width)
        grad_keys = accums[0].reshape(seq_len, width).astype(jnp.bfloat16)
        grad_values = accums[1].reshape(seq_len, width).astype(jnp.bfloat16)
        frames_part = (
            contract(grad_query, attn_full[0], 1, 1)
            + contract(grad_keys, attn_full[1], 1, 1)
            + contract(grad_values, attn_full[2], 1, 1)
        )
        rows_grad = grad_one + lax.psum_scatter(
            frames_part.astype(jnp.bfloat16), "tensor", scatter_dimension=0, tiled=True
        ).astype(jnp.float32)
        attn_grads = jnp.stack(
            [
                contract(frames_all, grad_query, 0, 0),
                contract(frames_all, grad_keys, 0, 0),
                contract(frames_all, grad_values, 0, 0),
                grad_proj,
            ]
        )
        ffn_grads = jnp.stack([grad_up, grad_down])
        small_grads = jnp.concatenate(
            [
                jnp.zeros((2 * D,), jnp.float32),
                jnp.sum(grad_one, 0),
                jnp.sum(grad_two, 0),
                grad_gain_one,
                grad_shift_one,
                grad_gain_two,
                grad_shift_two,
                jnp.zeros((FF,), jnp.float32),
            ]
        )
        small_grads = small_grads + place(
            jnp.sum(grad_query.astype(jnp.float32), 0), tensor_index * width
        )
        small_grads = small_grads + place(
            jnp.sum(grad_values.astype(jnp.float32), 0), D + tensor_index * width
        )
        small_grads = small_grads + place(jnp.sum(inner_grad, 0), 8 * D + tensor_index * ff_width)
        result = (result.astype(jnp.bfloat16), rows_grad, attn_grads, ffn_grads, small_grads)
        step_out = [result[0]]
        step_grad = [result[1]]
        step_attn = result[2]
        step_ffn = result[3]
        small_total = small_total + result[4]
        output_rows.append(jnp.stack(step_out))
        grad_rows_all.append(jnp.stack(step_grad))
        attn_shard = attn_shard + lax.psum_scatter(step_attn, "dp", scatter_dimension=1, tiled=True)
        ffn_shard = ffn_shard + lax.psum_scatter(step_ffn, "dp", scatter_dimension=1, tiled=True)
    count_part = jnp.sum(jnp.clip(lengths - tensor_index * half, 0, half)).astype(jnp.float32)
    square_part = jnp.sum(attn_shard * attn_shard) + jnp.sum(ffn_shard * ffn_shard)
    square_sum, small_sum, frame_count = lax.psum(
        (square_part, small_total, count_part), ("dp", "tensor")
    )
    grad_norm = jnp.sqrt(square_sum + jnp.sum(small_sum * small_sum)) / frame_count
    factor = jnp.minimum(1.0, CLIP_NORM / grad_norm) / frame_count
    attn_rates = RATE * jnp.array([1.0, 1.0, 1.0, 0.5 * SEQ**0.5], jnp.float32)[:, None, None]
    attn_new, attn_m_new, attn_v_new = adamw(
        attn_w, attn_m, attn_v, attn_shard * factor, attn_rates, DECAY
    )
    ffn_new, ffn_m_new, ffn_v_new = adamw(ffn_w, ffn_m, ffn_v, ffn_shard * factor, RATE, DECAY)
    small_new, small_m_new, small_v_new = adamw(
        small_w, small_m, small_v, small_sum * factor, SMALL_RATE, 0.0
    )
    return (
        jnp.stack(output_rows),
        jnp.stack(grad_rows_all),
        grad_norm,
        attn_new,
        attn_m_new,
        attn_v_new,
        ffn_new,
        ffn_m_new,
        ffn_v_new,
        small_new,
        small_m_new,
        small_v_new,
    )


def solution(mesh):
    in_specs = (
        P(None, "dp", "tensor", None),
        P(None, "dp", "tensor", None),
        P(None, "dp"),
        P(None, "dp", "tensor"),
        P(None, "dp", "tensor"),
        P(None, "dp", "tensor"),
        P(None, "dp", "tensor"),
        P(None, "dp", "tensor"),
        P(None, "dp", "tensor"),
        P(),
        P(),
        P(),
    )
    out_specs = (
        P(None, "dp", "tensor", None),
        P(None, "dp", "tensor", None),
        P(),
        P(None, "dp", "tensor"),
        P(None, "dp", "tensor"),
        P(None, "dp", "tensor"),
        P(None, "dp", "tensor"),
        P(None, "dp", "tensor"),
        P(None, "dp", "tensor"),
        P(),
        P(),
        P(),
    )
    return jax.shard_map(
        per_device, mesh=mesh, in_specs=in_specs, out_specs=out_specs, check_vma=False
    )
```

profile of v0, /device:TPU:0, one launch (start us, length us, event | category | flops | bytes accessed | tf_op | source)
XLA Modules:
  0.0 754.2 jit_solution(7644402040800725788)
XLA Ops:
  7.2 1.6 convert_element_type.254
  12.9 2.4 all-gather
  15.4 61.0 %all-gather.5.cloned.1.call-done = bf16[4,768,384]{2,1,0:T(8,128)(2,1)} async-done(((bf16[4,48,384]{2,1,0:T(8,128)(2,1)}), bf16[4,768,384]{2,1,0:T(8,128)(2,1)}) %all-gather.5.cloned.1.call-update) | async-done | bytes 2359312 | tf_op jit(solution)/shard_map/all_gather | solution.py:98
  76.4 1.6 convolution_convert_fusion.3
  78.0 1.7 fusion.35
  79.7 1.5 fusion.116
  82.2 2.5 copy-done.5
  86.5 1.8 fusion.90
  89.0 2.4 all-gather.1
  92.9 1.5 fusion.117
  95.4 1.7 copy-done.1
  99.1 1.8 fusion.89
  100.9 1.8 convert_element_type.262
  103.2 5.8 reduce-scatter.14.cloned.1.call-done
  109.0 1.9 fusion.108
  112.1 2.5 all_gather.34
  114.6 2.4 all_gather.37
  116.9 76.9 %all-gather.7.cloned.1.call-done = bf16[2,768,1536]{2,1,0:T(8,128)(2,1)} async-done(((bf16[2,48,1536]{2,1,0:T(8,128)(2,1)}), bf16[2,768,1536]{2,1,0:T(8,128)(2,1)}) %all-gather.7.cloned.1.call-update) | async-done | bytes 4718608 | tf_op jit(solution)/shard_map/all_gather | solution.py:99
  193.8 11.1 %multiply_convert_fusion.3 = (bf16[512,1536]{1,0:T(8,128)(2,1)S(1)}, f32[512,1536]{1,0:T(8,128)}, f32[512,1536]{1,0:T(8,128)}) fusion(f32[1536]{0:T(1024)S(1)} %dynamic_slice.29, bf16[512,768]{1,0:T(8,128)(2,1)} %all_gather.34, bf16[2,768,1536]{2,1,0:T(8,128)(2,1)} %all-gather.7.cloned.1.call-done), kind=kOutput, calls=%fused_computation.47 | convolution fusion | flops 1259864064 | bytes 11016192 | tf_op jit(solution)/shard_map/dot_general | solution.py:26
  206.1 2.3 fusion.30
  208.5 10.8 %multiply_convert_fusion.2 = (bf16[512,1536]{1,0:T(8,128)(2,1)S(1)}, f32[512,1536]{1,0:T(8,128)}, f32[512,1536]{1,0:T(8,128)}) fusion(f32[1536]{0:T(1024)S(1)} %dynamic_slice.29, bf16[512,768]{1,0:T(8,128)(2,1)S(1)} %all_gather.37, bf16[2,768,1536]{2,1,0:T(8,128)(2,1)} %all-gather.7.cloned.1.call-done), kind=kOutput, calls=%fused_computation.34 | convolution fusion | flops 1259864064 | bytes 11016192 | tf_op jit(solution)/shard_map/dot_general | solution.py:26
  220.4 4.0 fusion.31
  226.2 5.2 reduce-scatter.16.cloned.1.call-done
  231.5 1.8 fusion.106
  233.8 1.3 fusion.63
  235.2 1.7 fusion.105
  237.9 2.4 all_gather.38
  240.3 3.0 fusion.118
  244.6 2.3 fusion.32
  247.1 2.4 all_gather.40
  249.4 6.6 fusion.119
  257.2 4.0 fusion.33
  262.0 8.8 %reduce-scatter.22.cloned.1.call-done = bf16[256,768]{1,0:T(8,128)(2,1)} async-done(((bf16[512,768]{1,0:T(8,128)(2,1)}), bf16[256,768]{1,0:T(8,128)(2,1)}) %reduce-scatter.22.cloned.1.call-update) | async-done | bytes 393232 | tf_op jit(solution)/shard_map/reduce_scatter | solution.py:170
  270.8 3.0 multiply_reduce_fusion.3
  275.2 3.6 fusion.102
  279.5 2.5 all_gather.41
  282.0 1.9 convolution_convert_fusion
  284.0 1.4 multiply_reduce_fusion
  285.4 1.9 multiply_convert_fusion
  289.7 1.8 convert_reduce_fusion
  292.7 1.5 add_convert_fusion
  295.0 1.9 add_reduce_fusion.2
  296.9 2.6 all_gather.39
  300.4 4.7 multiply_reduce_fusion.1
  305.6 1.9 multiply_convert_fusion.1
  307.4 2.4 convert_reduce_fusion.3
  310.5 1.5 convolution_bitcast_fusion.5
  313.7 1.8 convert_reduce_fusion.2
  315.4 2.7 add_convert_fusion.1
  321.7 2.5 maximum_add_fusion.1
  324.1 6.6 copy.70
  332.4 1.4 convolution_bitcast_fusion.2
  333.9 1.4 convolution_bitcast_fusion.3
  335.5 1.4 convolution_bitcast_fusion
  337.2 1.4 convolution_bitcast_fusion.1
  338.6 5.1 maximum_add_fusion
  352.4 162.0 %all-reduce.4.cloned.1.call-done = f32[4,768,384]{2,0,1:T(4,128)} async-done(((f32[4,768,384]{2,0,1:T(4,128)}), f32[4,768,384]{2,0,1:T(4,128)}) %all-reduce.4.cloned.1.call-update) | async-done | bytes 4718608
  514.4 1.7 multiply_reduce_fusion.11
  516.2 175.1 %reduce-scatter.26.cloned.1.call-done = f32[2,48,1536]{2,1,0:T(8,128)} async-done(((f32[2,768,1536]{2,1,0:T(8,128)}), f32[2,48,1536]{2,1,0:T(8,128)}) %reduce-scatter.26.cloned.1.call-update) | async-done | bytes 589840 | tf_op jit(solution)/shard_map/reduce_scatter | solution.py:265
  691.3 1.9 multiply_reduce_fusion.10
  695.7 39.7 %all-reduce.1 = (f32[]{:T(128)}, f32[9216]{0:T(1024)S(1)}, f32[]{:T(128)}) all-reduce(f32[]{:T(128)S(6)} %add.422, f32[9216]{0:T(1024)} %add.433, f32[]{:T(128)S(6)} %convert_element_type.325), channel_id=1, replica_groups=mesh['dp'=16,'tensor'=2] {'dp','tensor'}, use_global_device_ids=true, to_apply=%region_36.37 | all-reduce | flops 9218 | bytes 73744 | tf_op jit(solution)/shard_map/psum | solution.py:268
  739.4 1.5 multiply_subtract_fusion.2
  740.9 2.1 multiply_subtract_fusion.1
  743.0 2.7 multiply_subtract_fusion
  (353 shorter events, 46.9 us)
Async XLA Ops:
  7.2 69.2 %all-gather.5.cloned.1.call-start = ((), (), s32[]{:S(2)}) async-start(), calls=%async_computation.9 | async-start | bytes 2506752 | tf_op jit(solution)/shard_map/all_gather | solution.py:98
  8.9 94.3 %reduce-scatter.10.cloned.1.call-start = ((), (), s32[]{:S(2)}) async-start(), calls=%async_computation.10 | async-start | bytes 2359296 | tf_op jit(solution)/shard_map/reduce_scatter | solution.py:142
  15.4 66.8 %copy-start.2 = (bf16[1,1,512,768]{3,2,1,0:T(8,128)(2,1)}, bf16[1,1,512,768]{3,2,1,0:T(8,128)(2,1)S(1)}, u32[]{:S(2)}) copy-start(bf16[1,1,512,768]{3,2,1,0:T(8,128)(2,1)S(1)} %all-gather) | copy-start | bytes 2359300
  88.3 20.8 %reduce-scatter.14.cloned.1.call-start = ((), (), s32[]{:S(2)}) async-start(), calls=%async_computation.13 | async-start | bytes 2359296 | tf_op jit(solution)/shard_map/reduce_scatter | solution.py:142
  98.3 4.7 copy-start.69
  100.9 92.9 %all-gather.7.cloned.1.call-start = ((), (), s32[]{:S(2)}) async-start(), calls=%async_computation.11 | async-start | bytes 5013504 | tf_op jit(solution)/shard_map/all_gather | solution.py:99
  102.8 123.4 %reduce-scatter.12.cloned.1.call-start = ((), (), s32[]{:S(2)}) async-start(), calls=%async_computation.12 | async-start | bytes 1179648 | tf_op jit(solution)/shard_map/reduce_scatter | solution.py:154
  103.1 128.3 %copy-start.70 = (f32[768]{0:T(1024)}, f32[768]{0:T(1024)S(1)}, u32[]{:S(2)}) copy-start(f32[768]{0:T(1024)S(1)} %get-tuple-element.204) | copy-start | bytes 9220
  110.9 120.5 %copy-start.73 = (f32[256]{0:T(256)}, f32[256]{0:T(256)S(1)}, u32[]{:S(2)}) copy-start(f32[256]{0:T(256)S(1)} %broadcast_multiply_fusion.3) | copy-start | bytes 3076
  111.2 120.3 %copy-start.74 = (f32[256]{0:T(256)}, f32[256]{0:T(256)S(1)}, u32[]{:S(2)}) copy-start(f32[256]{0:T(256)S(1)} %broadcast_multiply_fusion.1) | copy-start | bytes 3076
  111.7 93.2 %copy-start.100 = (f32[256]{0:T(256)}, f32[256]{0:T(256)S(1)}, u32[]{:S(2)}) copy-start(f32[256]{0:T(256)S(1)} %multiply_reduce_fusion.7) | copy-start | bytes 3076
  111.7 119.7 %copy-start.75 = (f32[256]{0:T(256)}, f32[256]{0:T(256)S(1)}, u32[]{:S(2)}) copy-start(f32[256]{0:T(256)S(1)} %fusion.93) | copy-start | bytes 3076
  111.7 119.7 %copy-start.76 = (f32[256]{0:T(256)}, f32[256]{0:T(256)S(1)}, u32[]{:S(2)}) copy-start(f32[256]{0:T(256)S(1)} %fusion.95) | copy-start | bytes 3076
  116.9 91.5 %copy-start.19 = (bf16[512,768]{1,0:T(8,128)(2,1)}, bf16[512,768]{1,0:T(8,128)(2,1)S(1)}, u32[]{:S(2)}) copy-start(bf16[512,768]{1,0:T(8,128)(2,1)S(1)} %all_gather.37) | copy-start | bytes 2359300
  193.8 12.3 %copy-start.105 = (bf16[2,768,1536]{2,1,0:T(8,128)(2,1)S(1)}, bf16[2,768,1536]{2,1,0:T(8,128)(2,1)}, u32[]{:S(2)}) copy-start(bf16[2,768,1536]{2,1,0:T(8,128)(2,1)} %all-gather.7.cloned.1.call-done) | copy-start | bytes 14155780
  208.4 23.0 %reduce-scatter.16.cloned.1.call-start = ((), (), s32[]{:S(2)}) async-start(), calls=%async_computation.14 | async-start | bytes 1179648 | tf_op jit(solution)/shard_map/reduce_scatter | solution.py:154
  224.4 9.4 %copy-start.30 = (bf16[2,1,256,768]{3,2,1,0:T(8,128)(2,1)S(1)}, bf16[2,1,256,768]{3,2,1,0:T(8,128)(2,1)}, u32[]{:S(2)}) copy-start(bf16[2,1,256,768]{3,2,1,0:T(8,128)(2,1)} %param.14) | copy-start | bytes 2359300
  224.4 37.5 %reduce-scatter.18.cloned.1.call-start = ((), (), s32[]{:S(2)}) async-start(), calls=%async_computation.15 | async-start | bytes 1179648 | tf_op jit(solution)/shard_map/reduce_scatter | solution.py:170
  231.5 8.8 %slice-start.4 = ((s8[4718592]{0:T(1024)(128)(4,1)}), s8[4194304]{0:T(1024)(128)(4,1)S(1)}, s32[]{:S(2)}) async-start(s8[4718592]{0:T(1024)(128)(4,1)} %bitcast.279), calls=%async_computation.25 | async-start | bytes 8388608
  233.8 6.5 slice-start.5
  235.2 5.1 copy-start.107
  235.2 5.1 copy-start.108
  236.9 6.4 copy-start.93
  246.9 23.9 %reduce-scatter.22.cloned.1.call-start = ((), (), s32[]{:S(2)}) async-start(), calls=%async_computation.17 | async-start | bytes 1179648 | tf_op jit(solution)/shard_map/reduce_scatter | solution.py:170
  246.9 9.1 %copy-start.94 = (f32[256]{0:T(256)}, f32[256]{0:T(256)S(1)}, u32[]{:S(2)}) copy-start(f32[256]{0:T(256)S(1)} %negate_multiply_fusion.3) | copy-start | bytes 3076
  249.4 6.6 copy-start.24
  257.2 4.7 copy-start.68
  257.2 4.7 copy-start.72
  261.2 88.8 %reduce-scatter.24.cloned.1.call-start = ((), (), s32[]{:S(2)}) async-start(), calls=%async_computation.18 | async-start | bytes 1179648 | tf_op jit(solution)/shard_map/reduce_scatter | solution.py:225
  262.0 13.2 %copy-start.57 = (bf16[256,768]{1,0:T(8,128)(2,1)S(1)}, bf16[256,768]{1,0:T(8,128)(2,1)}, u32[]{:S(2)}) copy-start(bf16[256,768]{1,0:T(8,128)(2,1)} %reduce-scatter.18.cloned.1.call-done) | copy-start | bytes 1179652
  270.8 13.1 %slice-start.2 = ((s8[6291456]{0:T(1024)(128)(4,1)}), s8[4194304]{0:T(1024)(128)(4,1)S(1)}, s32[]{:S(2)}) async-start(s8[6291456]{0:T(1024)(128)(4,1)} %bitcast.245), calls=%async_computation.23 | async-start | bytes 8388608
  275.2 8.8 %slice-start.3 = ((s8[6291456]{0:T(1024)(128)(4,1)}), s8[2097152]{0:T(1024)(128)(4,1)S(1)}, s32[]{:S(2)}) async-start(s8[6291456]{0:T(1024)(128)(4,1)} %bitcast.245), calls=%async_computation.24 | async-start | bytes 4194304
  278.8 5.2 copy-start.8
  278.8 5.2 copy-start.64
  278.8 5.2 copy-start.65
  278.8 5.2 copy-start.95
  294.3 56.9 %reduce-scatter.20.cloned.1.call-start = ((), (), s32[]{:S(2)}) async-start(), calls=%async_computation.16 | async-start | bytes 1179648 | tf_op jit(solution)/shard_map/reduce_scatter | solution.py:225
  294.3 6.0 copy-start.62
  295.0 10.0 %copy-start.97 = (f32[256]{0:T(256)}, f32[256]{0:T(256)S(1)}, u32[]{:S(2)}) copy-start(f32[256]{0:T(256)S(1)} %negate_multiply_fusion.4) | copy-start | bytes 3076
  300.3 4.7 copy-start.37
  300.3 4.7 slice-start
  300.4 5.2 slice-start.1
  318.2 196.3 %all-reduce.4.cloned.1.call-start = ((), (), s32[]{:S(2)}) async-start(), calls=%async_computation.20 | async-start | bytes 9437184
  330.8 360.5 %reduce-scatter.26.cloned.1.call-start = ((), (), s32[]{:S(2)}) async-start(), calls=%async_computation.19 | async-start | bytes 10027008 | tf_op jit(solution)/shard_map/reduce_scatter | solution.py:265
  343.7 4.5 copy-start.85
  343.7 4.5 copy-start.84
  343.7 4.5 copy-start.80
  343.8 4.5 copy-start.79
  343.8 4.5 copy-start.89
  343.8 4.5 copy-start.83
  343.8 4.5 copy-start.82
  343.8 4.5 copy-start.81
  343.8 4.6 copy-start.78
  343.8 4.6 copy-start.77
  343.8 5.1 copy-start.101
  343.8 5.3 copy-start.102
  343.9 6.2 copy-start.9
  343.9 6.1 copy-start.96
  343.9 7.3 copy-start.7
  343.9 7.3 copy-start.98
  351.2 389.7 %copy-start.60 = (f32[4,48,384]{2,1,0:T(8,128)S(1)}, f32[4,48,384]{2,1,0:T(8,128)}, u32[]{:S(2)}) copy-start(f32[4,48,384]{2,1,0:T(8,128)} %param.16) | copy-start | bytes 884740
  351.2 389.7 %copy-start.104 = (f32[4]{0:T(128)S(1)}, f32[4]{0:T(128)}, u32[]{:S(2)}) copy-start(f32[4]{0:T(128)} %constant.228) | copy-start | bytes 52
  516.2 226.8 %copy-start.32 = (f32[2,48,1536]{2,1,0:T(8,128)S(1)}, f32[2,48,1536]{2,1,0:T(8,128)}, u32[]{:S(2)}) copy-start(f32[2,48,1536]{2,1,0:T(8,128)} %param.19) | copy-start | bytes 1769476
  691.3 51.7 %copy-start.33 = (f32[2,48,1536]{2,1,0:T(8,128)S(1)}, f32[2,48,1536]{2,1,0:T(8,128)}, u32[]{:S(2)}) copy-start(f32[2,48,1536]{2,1,0:T(8,128)} %reduce-scatter.26.cloned.1.call-done) | copy-start | bytes 1769476
  (63 other events, 144.0 us)
Sparse Core Ops, SparseCore 0:
  11.3 65.0 all-gather.4
  88.4 7.8 reduce-scatter.9
  101.0 7.9 reduce-scatter.13
  112.1 81.6 all-gather.6
  208.6 6.8 reduce-scatter.11
  224.5 6.8 reduce-scatter.15
  247.0 9.4 reduce-scatter.17
  261.4 9.3 reduce-scatter.21
  294.4 9.4 reduce-scatter.23
  318.3 9.4 reduce-scatter.19
  333.5 180.8 all-reduce.3
  520.9 170.3 reduce-scatter.25
where the time goes:
time: 764 us; the launch traced here: 754 us
  waiting for transfers between devices  495 us (65%)
  matrix products  93.1 us (12%)
  blocking collectives  59.2 us (8%)
  other arithmetic  56.4 us (7%)
  local copies, waits for them, and re-layouts  25.4 us (3%)
  between operations  23.5 us (3%)
    reduce_scatter x1, waiting for transfers between devices, per_device(): lax.psum_scatter(step_ffn, 'dp', scatter_dimension=1, tiled=True)  175 us
    unnamed x13, waiting for transfers between devices  162 us
    all_gather x1, waiting for transfers between devices, per_device(): lax.all_gather(ffn_w.astype(jnp.bfloat16), 'dp', axis=1, tiled=True)  76.9 us
    all_gather x1, waiting for transfers between devices, per_device(): lax.all_gather(attn_w.astype(jnp.bfloat16), 'dp', axis=1, tiled=True)  61 us
    psum x1, blocking collectives, per_device(): lax.psum((square_part, small_total, count_part), ('dp', 'tensor'))  39.7 us
    dot_general x12, matrix products, matmul(): return jnp.dot(left, right, preferred_element_type=jnp.float32)  39.2 us
    dot_general x24, matrix products, contract(): lax.dot_general(left, right, (((left_dim,), (right_dim,)), ((), ())), pre...  33.1 us
  transfers between devices with their start and end apart: 12, of which 7 were waited for; matrix products, arithmetic and copies ran while one was open for 13% of the time, Pallas kernels for 0%

commit v1 on v0

v1 whole, which is shorter than its diff:
```python
import functools
import math

import jax
import jax.numpy as jnp
from jax import lax
from jax.experimental import pallas as pl
from jax.experimental.pallas import tpu as pltpu
from jax.sharding import PartitionSpec as P

HD = 64
D = 768
FF = 3072
SEQ = 512
HALF = SEQ // 2
STEP = 10
SMALL = 9216
PAIRS = 6
BLOCKS = 16
ROWS = D // BLOCKS

EPS_NORM = 1e-05
MASK_FILL = -1e30
BETA_ONE = 0.9
BETA_TWO = 0.999
ADAM_EPS = 1e-08
CLIP_NORM = 0.1
RATE = 0.1
SMALL_RATE = 1.5
DECAY = 0.01

BF = jnp.bfloat16
F32 = jnp.float32

STEP_A = (2, 1)
STEP_B = (1, 2)
Z_MASKS = (0, 4, 8, 12)
MASKS = tuple(
    (
        tuple(z for z in Z_MASKS) + tuple(z + near for z in Z_MASKS),
        tuple(z + far for z in Z_MASKS) + tuple(z + near + far for z in Z_MASKS),
    )
    for near, far in (STEP_A, STEP_B)
)


def dot(left, right):
    return jnp.dot(left, right, preferred_element_type=F32)


def dot_t(left, right):
    return lax.dot_general(left, right, (((1,), (1,)), ((), ())), preferred_element_type=F32)


ERF_P = 0.35
ERF_Q = (
    0.19402205421243862,
    0.2385478098291166,
    -0.017756407016771347,
    0.7010874955540375,
    -0.6969262406496157,
    0.7808055624011503,
    -0.1997802807385829,
)


def gelu_pair(u):
    t = 1.0 / (1.0 + (ERF_P * math.sqrt(0.5)) * jnp.abs(u))
    bell = jnp.exp(-0.5 * u * u)
    acc = ERF_Q[6] * t + ERF_Q[5]
    for k in (4, 3, 2, 1, 0):
        acc = acc * t + ERF_Q[k]
    tail = 0.5 * (acc * t) * bell
    phi = jnp.where(u >= 0.0, 1.0 - tail, tail)
    return u * phi, phi + (u * bell) * (1.0 / math.sqrt(2.0 * math.pi))


def spec(kind):
    if kind == "s":
        return pl.BlockSpec(memory_space=pltpu.SMEM)
    if kind == "v":
        return pl.BlockSpec(memory_space=pltpu.VMEM)
    return pl.BlockSpec(memory_space=pl.ANY)


def kernel_call(body, name, in_kinds, outs, scratch, vmem_mib, flops, moved):
    return pl.pallas_call(
        body,
        name=name,
        in_specs=[spec(k) for k in in_kinds],
        out_specs=[spec(k) for k, _, _ in outs],
        out_shape=[jax.ShapeDtypeStruct(s, d) for _, s, d in outs],
        scratch_shapes=scratch,
        compiler_params=pltpu.CompilerParams(vmem_limit_bytes=vmem_mib * 2**20),
        cost_estimate=pl.CostEstimate(flops=flops, bytes_accessed=moved, transcendentals=0),
    )


W_SHAPE = (4, D, D)


def place_start(meta, pieces, w, sems):
    d = meta[0]
    for part in range(4):
        rel, half = divmod(part, 2)
        for sel in range(2):
            src = pieces[half * 4 + rel * 2 + sel]
            for j in range(8):
                row = pl.multiple_of((d ^ MASKS[half][sel][j]) * ROWS, 16)
                pltpu.make_async_copy(
                    src.at[j], w.at[part, pl.ds(row, ROWS)], sems.at[part]
                ).start()


def place_wait(w, sems, part):
    pltpu.make_async_copy(w.at[part], w.at[part], sems.at[part]).wait()


def attn_fwd_body(meta, xo, xr, *refs):
    pieces = refs[:8]
    s12, s24 = refs[8:10]
    q_ref, k_ref, v_ref, p_out, ot_ref, o0, o1, yh_ref, rs_ref, hb_ref = refs[10:20]
    w, p_buf, w_sems, p_sems = refs[20:]
    place_start(meta, pieces, w, w_sems)
    t, length = meta[1], meta[2]
    for rel in range(2):
        h = t ^ rel
        place_wait(w, w_sems, rel * 2)
        place_wait(w, w_sems, rel * 2 + 1)
        bq = s24[pl.ds(h, 1), :]
        bv = s24[pl.ds(2 + h, 1), :]
        for r, x in ((0, xo), (1, xr)):
            rows = pl.ds(r * HALF, HALF)
            qk = dot(x[...], w[rel * 2])
            q = (qk[:, :384] + bq).astype(BF) * jnp.asarray(HD**-0.5, BF)
            k = qk[:, 384:].astype(BF)
            v = (dot(x[...], w[rel * 2 + 1, :, :384]) + bv).astype(BF)
            for i in range(3):
                cols = slice(i * 128, (i + 1) * 128)
                q_ref[rel * 3 + i, rows, :] = q[:, cols]
                k_ref[rel * 3 + i, rows, :] = k[:, cols]
                v_ref[rel * 3 + i, rows, :] = v[:, cols]
    row = lax.broadcasted_iota(jnp.int32, (SEQ, 1), 0)
    first = row < HALF
    position = jnp.where(first, row + t * HALF, row + (1 - t) * HALF - HALF)
    valid = position < length
    lane = lax.broadcasted_iota(jnp.int32, (SEQ, 128), 1)
    for rel in range(2):
        o_ref = (o0, o1)[rel]

        def pair(i, carry, rel=rel, o_ref=o_ref):
            p = rel * 3 + i
            keys = k_ref[p]
            q_t = q_ref[p].T
            v_t = v_ref[p].T
            halves = []
            for hh in range(2):
                own = (lane < HD) if hh == 0 else (lane >= HD)
                s = dot(jnp.where(own, keys, jnp.zeros_like(keys)), q_t)
                s = jnp.where(valid, s, MASK_FILL)
                e = jnp.exp(s - jnp.max(s, 0, keepdims=True))
                prob = (e * (1.0 / jnp.sum(e, 0, keepdims=True))).astype(BF)
                p_buf[2 * p + hh] = prob
                pltpu.make_async_copy(
                    p_buf.at[2 * p + hh], p_out.at[2 * p + hh], p_sems.at[2 * p + hh]
                ).start()
                halves.append(dot(v_t[hh * HD : (hh + 1) * HD], prob))
            o_t = jnp.concatenate(halves, 0).astype(BF)
            ot_ref[p] = o_t
            o_ref[:, pl.ds(pl.multiple_of(i * 128, 128), 128)] = o_t.T
            return carry

        lax.fori_loop(0, 3, pair, 0)
    bo, g1, c1 = s12[2:3, :], s12[4:5, :], s12[5:6, :]
    for r, x in ((0, xo), (1, xr)):
        rows = pl.ds(r * HALF, HALF)
        a = dot_t(o0[rows, :], w[1, :, 384:]) + dot_t(o1[rows, :], w[3, :, 384:])
        y = x[...].astype(F32) + a + bo
        centred = y - jnp.mean(y, -1, keepdims=True)
        inv = lax.rsqrt(jnp.mean(centred * centred, -1, keepdims=True) + EPS_NORM)
        hat = centred * inv
        yh_ref[rows, :] = hat
        rs_ref[rows, :] = inv
        hb_ref[rows, :] = (hat * g1 + c1).astype(BF)
    for i in range(12):
        pltpu.make_async_copy(p_buf.at[i], p_out.at[i], p_sems.at[i]).wait()


def attn_fwd(meta, xo, xr, pieces, s12, s24):
    return kernel_call(
        attn_fwd_body,
        "attn_fwd",
        "svv" + "a" * 8 + "vv",
        [
            ("v", (PAIRS, SEQ, 128), BF),
            ("v", (PAIRS, SEQ, 128), BF),
            ("v", (PAIRS, SEQ, 128), BF),
            ("a", (12, SEQ, SEQ), BF),
            ("v", (PAIRS, 128, SEQ), BF),
            ("v", (SEQ, 384), BF),
            ("v", (SEQ, 384), BF),
            ("v", (SEQ, D), F32),
            ("v", (SEQ, 1), F32),
            ("v", (SEQ, D), BF),
        ],
        [
            pltpu.VMEM(W_SHAPE, BF),
            pltpu.VMEM((12, SEQ, SEQ), BF),
            pltpu.SemaphoreType.DMA((4,)),
            pltpu.SemaphoreType.DMA((12,)),
        ],
        40,
        6 * 10**9,
        20 * 10**6,
    )(meta, xo, xr, *pieces, s12, s24)


CHUNK = 256
PER_PART = D // CHUNK


def chunk_of(c):
    return pl.ds(pl.multiple_of((c % PER_PART) * CHUNK, CHUNK), CHUNK)


def ffn_up_body(meta, hb, *refs):
    pieces = refs[:8]
    b1, f0, f1, gp, w, sems = refs[8:]
    c = pl.program_id(0)

    @pl.when(c == 0)
    def _():
        place_start(meta, pieces, w, sems)

    part = c // PER_PART

    @pl.when(c % PER_PART == 0)
    def _():
        place_wait(w, sems, part)

    u = dot(hb[...], w[part, :, chunk_of(c)]) + b1[0]
    f, slope = gelu_pair(u)
    gp[0] = slope.astype(BF)

    @pl.when(part < 2)
    def _():
        f0[...] = f.astype(BF)

    @pl.when(part >= 2)
    def _():
        f1[...] = f.astype(BF)


N_CHUNKS = FF // CHUNK
SIDE = N_CHUNKS // 2


def grid_call(body, name, in_specs, out_specs, out_shape, scratch, vmem_mib, flops, moved):
    return pl.pallas_call(
        body,
        name=name,
        grid_spec=pltpu.PrefetchScalarGridSpec(
            num_scalar_prefetch=1,
            grid=(N_CHUNKS,),
            in_specs=in_specs,
            out_specs=out_specs,
            scratch_shapes=scratch,
        ),
        out_shape=out_shape,
        compiler_params=pltpu.CompilerParams(
            vmem_limit_bytes=vmem_mib * 2**20, dimension_semantics=("arbitrary",)
        ),
        cost_estimate=pl.CostEstimate(flops=flops, bytes_accessed=moved, transcendentals=0),
    )


def whole(shape):
    return pl.BlockSpec(shape, lambda c, meta: (0,) * len(shape))


ANY = pl.BlockSpec(memory_space=pl.ANY)
SIDE_SPECS = [
    pl.BlockSpec((SEQ, CHUNK), lambda c, meta: (0, jnp.minimum(c, SIDE - 1))),
    pl.BlockSpec((SEQ, CHUNK), lambda c, meta: (0, jnp.maximum(c - SIDE, 0))),
]
BIAS_SPEC = pl.BlockSpec((1, 1, CHUNK), lambda c, meta: (meta[1] ^ (c // SIDE), 0, c % SIDE))
BOTH_SPEC = pl.BlockSpec((1, SEQ, CHUNK), lambda c, meta: (c // SIDE, 0, c % SIDE))


def ffn_up(meta, hb, pieces, b1):
    return grid_call(
        ffn_up_body,
        "ffn_up",
        [whole((SEQ, D))] + [ANY] * 8 + [BIAS_SPEC],
        SIDE_SPECS + [BOTH_SPEC],
        [
            jax.ShapeDtypeStruct((SEQ, FF // 2), BF),
            jax.ShapeDtypeStruct((SEQ, FF // 2), BF),
            jax.ShapeDtypeStruct((2, SEQ, FF // 2), BF),
        ],
        [pltpu.VMEM(W_SHAPE, BF), pltpu.SemaphoreType.DMA((4,))],
        24,
        5 * 10**9,
        12 * 10**6,
    )(meta, hb, *pieces, b1)


def norm_back(grad, hat, inv, gain):
    scaled = grad * gain
    return inv * (
        scaled
        - jnp.mean(scaled, -1, keepdims=True)
        - hat * jnp.mean(scaled * hat, -1, keepdims=True)
    )


def row_sum(v):
    return jnp.sum(v, 0, keepdims=True)


def ffn_down_body(meta, f0, f1, *refs):
    pieces = refs[:8]
    yh, co, cr, s12, out_o, out_r, dz, dy2, sums, w, sems = refs[8:]
    place_start(meta, pieces, w, sems)
    t, length = meta[1], meta[2]
    b2 = s12[3:4, :]
    g1, c1, g2, c2 = s12[4:5, :], s12[5:6, :], s12[6:7, :], s12[7:8, :]
    for part in range(4):
        place_wait(w, sems, part)
    totals = [jnp.zeros((1, D), F32)] * 3
    for r, cot, out in ((0, co, out_o), (1, cr, out_r)):
        rows = pl.ds(r * HALF, HALF)
        z = dot_t(f0[rows, :D], w[0])
        z = z + dot_t(f0[rows, D:], w[1])
        z = z + dot_t(f1[rows, :D], w[2])
        z = z + dot_t(f1[rows, D:], w[3])
        y = yh[rows, :] * g1 + c1 + z + b2
        centred = y - jnp.mean(y, -1, keepdims=True)
        inv = lax.rsqrt(jnp.mean(centred * centred, -1, keepdims=True) + EPS_NORM)
        hat = centred * inv
        out[...] = (hat * g2 + c2).astype(BF)
        row = lax.broadcasted_iota(jnp.int32, (HALF, 1), 0)
        valid = row + (t ^ r) * HALF < length
        dout = jnp.where(valid, cot[...].astype(F32), 0.0)
        grad = norm_back(dout, hat, inv, g2)
        dy2[rows, :] = grad
        dz[rows, :] = grad.astype(BF)
        totals = [
            a + row_sum(b) for a, b in zip(totals, (grad, dout * hat, dout), strict=True)
        ]
    for i in range(3):
        sums[i : i + 1, :] = totals[i]


def ffn_down(meta, f0, f1, pieces, yh, co, cr, s12):
    return kernel_call(
        ffn_down_body,
        "ffn_down",
        "svv" + "a" * 8 + "vvvv",
        [
            ("v", (HALF, D), BF),
            ("v", (HALF, D), BF),
            ("v", (SEQ, D), BF),
            ("v", (SEQ, D), F32),
            ("v", (8, D), F32),
        ],
        [pltpu.VMEM(W_SHAPE, BF), pltpu.SemaphoreType.DMA((4,))],
        28,
        3 * 10**9,
        12 * 10**6,
    )(meta, f0, f1, *pieces, yh, co, cr, s12)


def ffn_back_body(meta, dz, *refs):
    pieces = refs[:8]
    gp, du0, du1, db1, w, sems = refs[8:]
    c = pl.program_id(0)

    @pl.when(c == 0)
    def _():
        place_start(meta, pieces, w, sems)

    part = c // PER_PART

    @pl.when(c % PER_PART == 0)
    def _():
        place_wait(w, sems, part)

    du = dot(dz[...], w[part, :, chunk_of(c)]) * gp[0].astype(F32)
    db1[0] = row_sum(du)

    @pl.when(part < 2)
    def _():
        du0[...] = du.astype(BF)

    @pl.when(part >= 2)
    def _():
        du1[...] = du.astype(BF)


def ffn_back(meta, dz, pieces, gp):
    return grid_call(
        ffn_back_body,
        "ffn_back",
        [whole((SEQ, D))] + [ANY] * 8 + [BOTH_SPEC],
        SIDE_SPECS + [BIAS_SPEC],
        [
            jax.ShapeDtypeStruct((SEQ, FF // 2), BF),
            jax.ShapeDtypeStruct((SEQ, FF // 2), BF),
            jax.ShapeDtypeStruct((2, 1, FF // 2), F32),
        ],
        [pltpu.VMEM(W_SHAPE, BF), pltpu.SemaphoreType.DMA((4,))],
        24,
        3 * 10**9,
        12 * 10**6,
    )(meta, dz, *pieces, gp)


def hidden_back_body(meta, du0, du1, *refs):
    pieces = refs[:8]
    dy2, yh, inv, s12, dy1, da, sums, w, sems = refs[8:]
    place_start(meta, pieces, w, sems)
    g1 = s12[4:5, :]
    for part in range(4):
        place_wait(w, sems, part)
    totals = [jnp.zeros((1, D), F32)] * 3
    for r in range(2):
        rows = pl.ds(r * HALF, HALF)
        dh = dy2[rows, :] + dot_t(du0[rows, :D], w[0])
        dh = dh + dot_t(du0[rows, D:], w[1])
        dh = dh + dot_t(du1[rows, :D], w[2])
        dh = dh + dot_t(du1[rows, D:], w[3])
        hat = yh[rows, :]
        grad = norm_back(dh, hat, inv[rows, :], g1)
        dy1[rows, :] = grad
        da[rows, :] = grad.astype(BF)
        totals = [a + row_sum(b) for a, b in zip(totals, (grad, dh * hat, dh), strict=True)]
    for i in range(3):
        sums[i : i + 1, :] = totals[i]


def hidden_back(meta, du0, du1, pieces, dy2, yh, inv, s12):
    return kernel_call(
        hidden_back_body,
        "hidden_back",
        "svv" + "a" * 8 + "vvvv",
        [("v", (SEQ, D), F32), ("v", (SEQ, D), BF), ("v", (8, D), F32)],
        [pltpu.VMEM(W_SHAPE, BF), pltpu.SemaphoreType.DMA((4,))],
        28,
        3 * 10**9,
        12 * 10**6,
    )(meta, du0, du1, *pieces, dy2, yh, inv, s12)


def attn_back_body(meta, da, dy1, *refs):
    pieces = refs[:8]
    q_ref, k_ref, v_ref, p_in, ot_ref = refs[8:13]
    dq0, dk0, dv0, dq1, dk1, dv1, dx_o, dx_r, sums = refs[13:22]
    w, p_buf, do_ref, w_sems, p_sems = refs[22:]
    place_start(meta, pieces, w, w_sems)
    for i in range(12):
        pltpu.make_async_copy(p_in.at[i], p_buf.at[i], p_sems.at[i]).start()
    t = meta[1]
    for rel in range(2):
        place_wait(w, w_sems, rel * 2 + 1)
        do = dot(da[...], w[rel * 2 + 1, :, 384:]).astype(BF)
        for i in range(3):
            do_ref[rel * 3 + i] = do[:, i * 128 : (i + 1) * 128]
    lane = lax.broadcasted_iota(jnp.int32, (SEQ, 128), 1)
    low_lane = lane < HD
    for rel in range(2):
        dq_ref, dk_ref, dv_ref = ((dq0, dk0, dv0), (dq1, dk1, dv1))[rel]

        def pair(i, carry, rel=rel, dq_ref=dq_ref, dk_ref=dk_ref, dv_ref=dv_ref):
            p = rel * 3 + i
            dop = do_ref[p]
            qp = q_ref[p]
            vp = v_ref[p]
            k_t = k_ref[p].T
            do_t = dop.T
            both = do_t.astype(F32) * ot_ref[p].astype(F32)
            parts = []
            for hh in range(2):
                own = low_lane if hh == 0 else (lane >= HD)
                inside = slice(hh * HD, (hh + 1) * HD)
                delta = row_sum(both[inside])
                slope = dot(jnp.where(own, vp, jnp.zeros_like(vp)), do_t)
                pltpu.make_async_copy(
                    p_in.at[2 * p + hh], p_buf.at[2 * p + hh], p_sems.at[2 * p + hh]
                ).wait()
                prob = p_buf[2 * p + hh]
                ds = (prob.astype(F32) * (slope - delta)).astype(BF)
                parts.append((dot(prob, dop), dot(ds, qp), dot(k_t[inside], ds)))
            cols = pl.ds(pl.multiple_of(i * 128, 128), 128)
            dv_ref[:, cols] = jnp.where(low_lane, parts[0][0], parts[1][0]).astype(BF)
            dk_ref[:, cols] = jnp.where(low_lane, parts[0][1], parts[1][1]).astype(BF)
            dq_t = jnp.concatenate([parts[0][2], parts[1][2]], 0) * (HD**-0.5)
            dq_ref[:, cols] = dq_t.T.astype(BF)
            return carry

        lax.fori_loop(0, 3, pair, 0)
        h = t ^ rel
        sums[pl.ds(h, 1), :] = row_sum(dq_ref[...].astype(F32))
        sums[pl.ds(2 + h, 1), :] = row_sum(dv_ref[...].astype(F32))
    place_wait(w, w_sems, 0)
    place_wait(w, w_sems, 2)
    for r, dx in ((0, dx_o), (1, dx_r)):
        rows = pl.ds(r * HALF, HALF)
        total = dy1[rows, :]
        for rel in range(2):
            dq_ref, dk_ref, dv_ref = ((dq0, dk0, dv0), (dq1, dk1, dv1))[rel]
            total = total + dot_t(dq_ref[rows, :], w[rel * 2, :, :384])
            total = total + dot_t(dk_ref[rows, :], w[rel * 2, :, 384:])
            total = total + dot_t(dv_ref[rows, :], w[rel * 2 + 1, :, :384])
        dx[...] = total


def attn_back(meta, da, dy1, pieces, q, k, v, prob, o_t):
    return kernel_call(
        attn_back_body,
        "attn_back",
        "svv" + "a" * 8 + "vvvav",
        [("v", (SEQ, 384), BF)] * 6 + [("v", (HALF, D), F32)] * 2 + [("v", (8, 384), F32)],
        [
            pltpu.VMEM(W_SHAPE, BF),
            pltpu.VMEM((12, SEQ, SEQ), BF),
            pltpu.VMEM((PAIRS, SEQ, 128), BF),
            pltpu.SemaphoreType.DMA((4,)),
            pltpu.SemaphoreType.DMA((12,)),
        ],
        40,
        8 * 10**9,
        20 * 10**6,
    )(meta, da, dy1, *pieces, q, k, v, prob, o_t)


def put_out(meta, acc, outs, sems):
    d = meta[0]
    for half in range(2):
        for sel in range(2):
            out = outs[half * 2 + sel]
            for j in range(8):
                row = pl.multiple_of((d ^ MASKS[half][sel][j]) * ROWS, 16)
                pltpu.make_async_copy(
                    acc.at[half, pl.ds(row, ROWS)], out.at[j], sems.at[half]
                ).start()


def put_wait(acc, sems):
    for half in range(2):
        pltpu.make_async_copy(acc.at[half], acc.at[half], sems.at[half]).wait()


GRAD_OUTS = [("a", (8, ROWS, D), BF)] * 4


def ffn_grad_body(meta, left_o, left_r, right_o, right_r, *refs):
    outs = refs[:4]
    left_t, acc, sems = refs[4:]
    left_t[:, :SEQ] = left_o[...].T
    left_t[:, SEQ:] = left_r[...].T
    for half in range(2):
        cols = slice(half * D, (half + 1) * D)
        for m in range(3):
            rows = pl.ds(m * 256, 256)
            total = dot(left_t[rows, :SEQ], right_o[:, cols])
            total = total + dot(left_t[rows, SEQ:], right_r[:, cols])
            acc[half, rows, :] = total.astype(BF)
    put_out(meta, acc, outs, sems)
    put_wait(acc, sems)


def ffn_grad(meta, left_o, left_r, right_o, right_r):
    return kernel_call(
        ffn_grad_body,
        "ffn_grad",
        "svvvv",
        GRAD_OUTS,
        [
            pltpu.VMEM((D, 2 * SEQ), BF),
            pltpu.VMEM((2, D, D), BF),
            pltpu.SemaphoreType.DMA((2,)),
        ],
        24,
        3 * 10**9,
        8 * 10**6,
    )(meta, left_o, left_r, right_o, right_r)


def attn_grad_body(meta, xo, xr, zo, zr, dao, dar, *refs):
    dq0, dk0, dv0, oo, dqr, dkr, dvr, orr = refs[:8]
    outs = refs[8:12]
    x_t, da_t, acc, sems = refs[12:]
    x_t[:, :HALF] = xo[...].T
    x_t[:, HALF:SEQ] = xr[...].T
    x_t[:, SEQ : SEQ + HALF] = zo[...].T
    x_t[:, SEQ + HALF :] = zr[...].T
    da_t[:, :SEQ] = dao[...].T
    da_t[:, SEQ:] = dar[...].T
    for half, side, left_t, own, other in (
        (0, 0, x_t, dq0, dqr),
        (0, 1, x_t, dk0, dkr),
        (1, 0, x_t, dv0, dvr),
        (1, 1, da_t, oo, orr),
    ):
        for m in range(3):
            rows = pl.ds(m * 256, 256)
            total = dot(left_t[rows, :SEQ], own[...]) + dot(left_t[rows, SEQ:], other[...])
            acc[half, rows, side * 384 : (side + 1) * 384] = total.astype(BF)
    put_out(meta, acc, outs, sems)
    put_wait(acc, sems)


def attn_grad(meta, xs, das, own, other):
    return kernel_call(
        attn_grad_body,
        "attn_grad",
        "s" + "v" * 14,
        GRAD_OUTS,
        [
            pltpu.VMEM((D, 2 * SEQ), BF),
            pltpu.VMEM((D, 2 * SEQ), BF),
            pltpu.VMEM((2, D, D), BF),
            pltpu.SemaphoreType.DMA((2,)),
        ],
        24,
        3 * 10**9,
        8 * 10**6,
    )(meta, *xs, *das, *own, *other)


def adamw(weight, moment_one, moment_two, grad, rate, decay):
    new_one = BETA_ONE * moment_one + (1.0 - BETA_ONE) * grad
    new_two = BETA_TWO * moment_two + (1.0 - BETA_TWO) * grad * grad
    fixed_one = new_one / (1.0 - BETA_ONE**STEP)
    fixed_two = new_two / (1.0 - BETA_TWO**STEP)
    update = fixed_one / (jnp.sqrt(fixed_two) + ADAM_EPS) + decay * weight
    return (weight - rate * update, new_one, new_two)


def other_core(v):
    return lax.ppermute(v, "tensor", [(0, 1), (1, 0)])


def shift(v, mask, n):
    return lax.ppermute(v, "dp", [(i, i ^ mask) for i in range(n)])


def gather_half(block, half, n):
    near, far = (STEP_A, STEP_B)[half]
    own = jnp.stack([block] + [shift(block, z, n) for z in Z_MASKS[1:]])
    own = jnp.concatenate([own, shift(own, near, n)])
    far_side = shift(own, far, n)
    return [own, far_side, other_core(own), other_core(far_side)]


def gather(halves, n):
    if n == BLOCKS:
        return gather_half(halves[0], 0, n) + gather_half(halves[1], 1, n)
    result = []
    for half in range(2):
        full = lax.all_gather(halves[half], "dp", axis=0, tiled=True)
        blocks = full.reshape(BLOCKS, ROWS, D)
        own = [blocks[jnp.array(m)] for m in MASKS[half]]
        result += own + [other_core(v) for v in own]
    return result


def added(*parts):
    total = parts[0].astype(F32)
    for p in parts[1:]:
        total = total + p.astype(F32)
    return total


def scatter_half(keep, send, half, n):
    near, far = (STEP_A, STEP_B)[half]
    came = shift(send, far, n)
    send = added(keep[4:], came[4:]).astype(BF)
    keep = added(keep[:4], came[:4]).astype(BF)
    came = shift(send, near, n)
    sends = [added(keep[i], came[i]).astype(BF) for i in range(1, 4)]
    arrived = [shift(s, z, n) for s, z in zip(sends, Z_MASKS[1:], strict=True)]
    return added(keep[0], came[0], *arrived)


def scatter(pieces, n):
    result = []
    for half in range(2):
        keep, send = pieces[2 * half], pieces[2 * half + 1]
        if n == BLOCKS:
            result.append(scatter_half(keep, send, half, n))
            continue
        order = MASKS[half][0] + MASKS[half][1]
        back = [order.index(i) for i in range(BLOCKS)]
        full = jnp.concatenate([keep, send])[jnp.array(back)].reshape(D, D).astype(F32)
        result.append(lax.psum_scatter(full, "dp", scatter_dimension=0, tiled=True))
    return result


def total_over_all(v, n):
    if n != BLOCKS:
        return lax.psum(v, ("dp", "tensor"))
    v = v + other_core(v)
    for masks in ((1, 2, 3), (4, 8, 12)):
        a, b, c = [shift(v, m, n) for m in masks]
        v = (v + a) + (b + c)
    return v


def per_device(
    frames,
    cotangent,
    lengths,
    attn_w,
    attn_m,
    attn_v,
    ffn_w,
    ffn_m,
    ffn_v,
    small_w,
    small_m,
    small_v,
):
    n = lax.axis_size("dp")
    t = lax.axis_index("tensor")
    d = lax.axis_index("dp") if n == BLOCKS else 0
    length = lax.dynamic_index_in_dim(lengths[:, 0], t, 0, keepdims=False)
    meta = jnp.stack([jnp.asarray(d, jnp.int32), jnp.asarray(t, jnp.int32), length])
    s12 = small_w.reshape(12, D)
    s24 = small_w.reshape(24, 384)
    b1 = small_w[8 * D :].reshape(2, 1, FF // 2)

    aw = attn_w.astype(BF)
    fw = ffn_w.astype(BF)
    attn_pieces = gather(
        [jnp.concatenate([aw[0], aw[1]], 1), jnp.concatenate([aw[2], aw[3]], 1)], n
    )
    up_pieces = gather([fw[0, :, :D], fw[0, :, D:]], n)
    down_pieces = gather([fw[1, :, :D], fw[1, :, D:]], n)

    def mine(v):
        return lax.dynamic_index_in_dim(v[:, 0], t, 0, keepdims=False)

    def theirs(v):
        return lax.dynamic_index_in_dim(v[:, 0], 1 - t, 0, keepdims=False)

    xo, zr = mine(frames), theirs(frames)
    xr = other_core(zr)
    zo = other_core(xo)
    co = mine(cotangent)
    cr = other_core(theirs(cotangent))

    q, k, v, prob, o_t, o0, o1, yh, inv, hb = attn_fwd(meta, xo, xr, attn_pieces, s12, s24)
    hb_r = other_core(hb)
    o_r = other_core(o1)
    f0, f1, gp = ffn_up(meta, hb, up_pieces, b1)
    f_r = other_core(f1)
    out_o, out_r, dz, dy2, sums_two = ffn_down(meta, f0, f1, down_pieces, yh, co, cr, s12)
    dz_r = other_core(dz)
    du0, du1, db1 = ffn_back(meta, dz, down_pieces, gp)
    du_r = other_core(du1)
    down_grads = scatter(ffn_grad(meta, dz, dz_r, f0, f_r), n)
    up_grads = scatter(ffn_grad(meta, hb, hb_r, du0, du_r), n)
    dy1, da, sums_one = hidden_back(meta, du0, du1, up_pieces, dy2, yh, inv, s12)
    da_r = other_core(da)
    early = jnp.concatenate(
        [
            sums_one[:1].reshape(-1),
            sums_two[:1].reshape(-1),
            sums_one[1:3].reshape(-1),
            sums_two[1:3].reshape(-1),
            db1.reshape(-1),
        ]
    )
    early = total_over_all(early, n)
    dq0, dk0, dv0, dq1, dk1, dv1, dx_o, dx_r, sums_qv = attn_back(
        meta, da, dy1, attn_pieces, q, k, v, prob, o_t
    )
    attn_grads = scatter(
        attn_grad(
            meta,
            (xo, xr, zo, zr),
            (da, da_r),
            (dq0, dk0, dv0, o0),
            (other_core(dq1), other_core(dk1), other_core(dv1), o_r),
        ),
        n,
    )

    def joined(own, other):
        return jnp.where(t == 0, jnp.stack([own, other]), jnp.stack([other, own]))[:, None]

    output = joined(out_o, other_core(out_r))
    frames_grad = joined(dx_o, other_core(dx_r))

    attn_g = jnp.stack(
        [
            attn_grads[0][:, :384],
            attn_grads[0][:, 384:],
            attn_grads[1][:, :384],
            attn_grads[1][:, 384:],
        ]
    )
    ffn_g = jnp.stack(
        [jnp.concatenate(up_grads, 1), jnp.concatenate(down_grads, 1)]
    )
    half = SEQ // lax.axis_size("tensor")
    count_part = jnp.sum(jnp.clip(lengths - t * half, 0, half)).astype(F32)
    square_part = sum(jnp.sum(g * g) for g in attn_grads + up_grads + down_grads)
    late = jnp.concatenate(
        [sums_qv[:4].reshape(-1), jnp.stack([square_part, count_part]), jnp.zeros((126,), F32)]
    )
    late = total_over_all(late, n)
    small_sum = jnp.concatenate([late[: 2 * D], early])
    square_sum, frame_count = late[2 * D], late[2 * D + 1]
    grad_norm = jnp.sqrt(square_sum + jnp.sum(small_sum * small_sum)) / frame_count
    factor = jnp.minimum(1.0, CLIP_NORM / grad_norm) / frame_count
    attn_rates = RATE * jnp.array([1.0, 1.0, 1.0, 0.5 * SEQ**0.5], F32)[:, None, None]
    attn_new, attn_m_new, attn_v_new = adamw(
        attn_w, attn_m, attn_v, attn_g * factor, attn_rates, DECAY
    )
    ffn_new, ffn_m_new, ffn_v_new = adamw(ffn_w, ffn_m, ffn_v, ffn_g * factor, RATE, DECAY)
    small_new, small_m_new, small_v_new = adamw(
        small_w, small_m, small_v, small_sum * factor, SMALL_RATE, 0.0
    )
    return (
        output,
        frames_grad,
        grad_norm,
        attn_new,
        attn_m_new,
        attn_v_new,
        ffn_new,
        ffn_m_new,
        ffn_v_new,
        small_new,
        small_m_new,
        small_v_new,
    )


def solution(mesh):
    rows = P(None, "dp", "tensor", None)
    weights = P(None, "dp", "tensor")
    in_specs = (rows, rows, P(None, "dp")) + (weights,) * 6 + (P(),) * 3
    out_specs = (rows, rows, P()) + (weights,) * 6 + (P(),) * 3
    return jax.shard_map(
        per_device, mesh=mesh, in_specs=in_specs, out_specs=out_specs, check_vma=False
    )
```

time: 764 us -> 402 us (0.53)
  waiting for transfers between devices: 495 us -> 80.2 us
  Pallas kernels: 0 us -> 114 us
  starting transfers between devices: 1.37 us -> 109 us
  matrix products: 93.1 us -> 0 us
  blocking collectives: 59.2 us -> 0 us
  local copies, waits for them, and re-layouts: 25.4 us -> 55.5 us
  other arithmetic: 56.4 us -> 26.8 us
  between operations: 23.5 us -> 11.4 us
    reduce_scatter x9 -> x0, waiting for transfers between devices: 195 us -> none  [the longest x1 175 us: per_device(): lax.psum_scatter(step_ffn, 'dp', scatter_dimension=1, tiled=True)]
    unnamed x13 -> x0, waiting for transfers between devices: 162 us -> none
    all_gather x2 -> x0, waiting for transfers between devices: 138 us -> none  [the longest x1 76.9 us: per_device(): lax.all_gather(ffn_w.astype(jnp.bfloat16), 'dp', axis=1, tiled=True)]
    pallas_call x0 -> x9, Pallas kernels: none -> 114 us  [the longest x1 21.3 us: attn_back(): kernel_call(attn_back_body, 'attn_back', 'svv' + 'a' * 8 + 'vvvav', [('v'...]
    ppermute x0 -> x100, starting transfers between devices: none -> 109 us  [the longest x72 104 us: shift(): return lax.ppermute(v, 'dp', [(i, i ^ mask) for i in range(n)])]
    dot_general x48 -> x0, matrix products: 93.1 us -> none  [the longest x12 39.2 us: matmul(): return jnp.dot(left, right, preferred_element_type=jnp.float32)]
    ppermute x0 -> x100, waiting for transfers between devices: none -> 80.2 us  [the longest x72 79 us: shift(): return lax.ppermute(v, 'dp', [(i, i ^ mask) for i in range(n)])]
    psum x1 -> x0, blocking collectives: 39.7 us -> none  [per_device(): lax.psum((square_part, small_total, count_part), ('dp', 'tensor'))]
  transfers between devices with their start and end apart: 12 -> 100, of which waited for: 7 -> 35; matrix products, arithmetic and copies ran while one was open for 13% -> 8% of each run, Pallas kernels for 0% -> 20%
where the time goes in v1:
time: 402 us; the launch traced here: 396 us
  Pallas kernels  114 us (28%)
  starting transfers between devices  109 us (27%)
  waiting for transfers between devices  80.2 us (20%)
  local copies, waits for them, and re-layouts  55.5 us (14%)
  other arithmetic  26.8 us (7%)
  between operations  11.4 us (3%)
    ppermute x72, starting transfers between devices, shift(): return lax.ppermute(v, 'dp', [(i, i ^ mask) for i in range(n)])  104 us
    ppermute x72, waiting for transfers between devices, shift(): return lax.ppermute(v, 'dp', [(i, i ^ mask) for i in range(n)])  79 us
    unnamed x242, local copies, waits for them, and re-layouts  44.1 us
    pallas_call x1, Pallas kernels, attn_back(): kernel_call(attn_back_body, 'attn_back', 'svv' + 'a' * 8 + 'vvvav', [('v'...  21.3 us
    pallas_call x1, Pallas kernels, attn_fwd(): kernel_call(attn_fwd_body, 'attn_fwd', 'svv' + 'a' * 8 + 'vv', [('v', (PA...  18.2 us
    pallas_call x1, Pallas kernels, ffn_up(): grid_call(ffn_up_body, 'ffn_up', [whole((SEQ, D))] + [ANY] * 8 + [BIAS_SP...  18.1 us
    pallas_call x2, Pallas kernels, ffn_grad(): kernel_call(ffn_grad_body, 'ffn_grad', 'svvvv', GRAD_OUTS, [pltpu.VMEM((D...  13.9 us
    pallas_call x1, Pallas kernels, ffn_back(): grid_call(ffn_back_body, 'ffn_back', [whole((SEQ, D))] + [ANY] * 8 + [BOT...  12.5 us
  transfers between devices with their start and end apart: 100, of which 35 were waited for; matrix products, arithmetic and copies ran while one was open for 8% of the time, Pallas kernels for 20%

profile of v1, /device:TPU:0, one launch (start us, length us, event | category | flops | bytes accessed | tf_op | source)
XLA Modules:
  0.0 396.3 jit_solution(17286026832962535725)
XLA Ops:
  2.4 3.0 collective-permute-start.8
  5.4 2.6 collective-permute-start.9
  9.6 3.5 collective-permute-start.2
  15.4 5.7 %collective-permute-start.16 = (bf16[48,768]{1,0:T(8,128)(2,1)S(1)}, bf16[48,768]{1,0:T(8,128)(2,1)S(1)}, u32[]{:S(2)}, u32[]{:S(2)}) collective-permute-start(bf16[48,768]{1,0:T(8,128)(2,1)S(1)} %copy-done.102), channel_id=1, source_target_pairs={{0,16},{2,18},{4,20},{6,22},{8,24},{10,26},{12,28},{14,30},{16,0},... | collective-permute-start | bytes 221192 | tf_op jit(solution)/shard_map/ppermute | solution.py:646
  22.3 3.5 collective-permute-start.23
  25.8 2.0 collective-permute-start.24
  28.6 5.4 %collective-permute-start.30 = (bf16[48,768]{1,0:T(8,128)(2,1)S(1)}, bf16[48,768]{1,0:T(8,128)(2,1)S(1)}, u32[]{:S(2)}, u32[]{:S(2)}) collective-permute-start(bf16[48,768]{1,0:T(8,128)(2,1)S(1)} %copy-done.98), channel_id=1, source_target_pairs={{0,16},{2,18},{4,20},{6,22},{8,24},{10,26},{12,28},{14,30},{16,0},... | collective-permute-start | bytes 221192 | tf_op jit(solution)/shard_map/ppermute | solution.py:646
  35.0 3.7 collective-permute-start.37
  38.7 1.5 collective-permute-start.11
  40.5 1.5 collective-permute-start.4
  42.7 2.7 collective-permute-done.11
  45.5 1.5 collective-permute-start.38
  47.1 3.4 collective-permute-done.4
  52.0 1.6 collective-permute-start.32
  54.1 2.7 collective-permute-done.18
  58.4 4.7 %collective-permute-done.32 = bf16[4,48,768]{2,1,0:T(8,128)(2,1)S(1)} collective-permute-done((bf16[4,48,768]{2,1,0:T(8,128)(2,1)S(1)}, bf16[4,48,768]{2,1,0:T(8,128)(2,1)S(1)}, u32[]{:S(2)}, u32[]{:S(2)}) %collective-permute-start.32) | collective-permute-done | bytes 294944 | tf_op jit(solution)/shard_map/ppermute | solution.py:646
  65.2 10.9 %collective-permute-done.39 = bf16[4,48,768]{2,1,0:T(8,128)(2,1)S(1)} collective-permute-done((bf16[4,48,768]{2,1,0:T(8,128)(2,1)S(1)}, bf16[4,48,768]{2,1,0:T(8,128)(2,1)S(1)}, u32[]{:S(2)}, u32[]{:S(2)}) %collective-permute-start.39) | collective-permute-done | bytes 294944 | tf_op jit(solution)/shard_map/ppermute | solution.py:646
  78.7 1.5 collective-permute-start.26
  84.4 8.7 %collective-permute-done.19.refs_1_ = bf16[8,48,768]{2,1,0:T(8,128)(2,1)S(1)} collective-permute-done((bf16[8,48,768]{2,1,0:T(8,128)(2,1)S(1)}, bf16[8,48,768]{2,1,0:T(8,128)(2,1)S(1)}, u32[]{:S(2)}, u32[]{:S(2)}) %collective-permute-start.19) | collective-permute-done | bytes 589856 | tf_op jit(solution)/shard_map/ppermute | solution.py:646
  93.1 1.5 collective-permute-start.40
  95.9 2.1 dynamic-slice_bitcast_fusion
  97.9 7.5 %collective-permute-done.33.refs_1_ = bf16[8,48,768]{2,1,0:T(8,128)(2,1)} collective-permute-done((bf16[8,48,768]{2,1,0:T(8,128)(2,1)}, bf16[8,48,768]{2,1,0:T(8,128)(2,1)}, u32[]{:S(2)}, u32[]{:S(2)}) %collective-permute-start.33) | collective-permute-done | bytes 589856 | tf_op jit(solution)/shard_map/ppermute | solution.py:646
  117.6 18.2 %attn_fwd.1 = (bf16[6,512,128]{2,1,0:T(8,128)(2,1)S(1)}, bf16[6,512,128]{2,1,0:T(8,128)(2,1)S(1)}, bf16[6,512,128]{2,1,0:T(8,128)(2,1)S(1)}, bf16[12,512,512]{2,...) custom-call(s32[3]{0:T(128)S(1)} %pad_add_fusion.meta, ...), custom_call_target="tpu_custom_call" | custom-call | flops 6000000000 | bytes 20000000 | tf_op jit(solution)/shard_map/attn_fwd/pallas_call | solution.py:190
  138.4 18.1 %ffn_up.1 = (bf16[512,1536]{1,0:T(8,128)(2,1)S(1)}, bf16[512,1536]{1,0:T(8,128)(2,1)}, bf16[2,512,1536]{2,1,0:T(8,128)(2,1)S(1)}) custom-call(s32[3]{0:T(128)S(1)} %pad_add_fusion.meta, bf16[512,768]{1,0:T(8,128)(2,1)S(1)} %get-tuple-element.57.hb.left_o, bf16[8,48,768]{2,1,0:T(8,128)(2,1)S(1)} %constant_dynamic-update-slice_fusion.10.refs_0_, ...), custom_call_target="tpu_custom_call" | custom-call | flops 5000000000 | bytes 12000000 | tf_op jit(solution)/shard_map/ffn_up/pallas_call | solution.py:291
  156.6 11.3 %ffn_down.1 = (bf16[256,768]{1,0:T(8,128)(2,1)S(1)}, bf16[256,768]{1,0:T(8,128)(2,1)S(1)}, bf16[512,768]{1,0:T(8,128)(2,1)S(1)}, f32[512,768]{1,0:T(8,128)S(1)}, f32[8,768]{1,0:T(8,128)S(1)}) custom-call(s32[3]{0:T(128)S(1)} %pad_add_fusion.meta, bf16[512,1536]{1,0:T(8,128)(2,1)S(1)} %get-tuple-element.58.f0.right_o, ...), custom_call_target="tpu_custom_call" | custom-call | flops 3000000000 | bytes 12000000 | tf_op jit(solution)/shard_map/ffn_down/pallas_call | solution.py:356
  168.0 12.5 %ffn_back.1 = (bf16[512,1536]{1,0:T(8,128)(2,1)S(1)}, bf16[512,1536]{1,0:T(8,128)(2,1)S(1)}, f32[2,1,1536]{2,1,0:T(1,128)S(1)}) custom-call(s32[3]{0:T(128)S(1)} %pad_add_fusion.meta, bf16[512,768]{1,0:T(8,128)(2,1)S(1)} %get-tuple-element.63.dz.left_o, bf16[8,48,768]{2,1,0:T(8,128)(2,1)S(1)} %copy-done.30, ...), custom_call_target="tpu_custom_call" | custom-call | flops 3000000000 | bytes 12000000 | tf_op jit(solution)/shard_map/ffn_back/pallas_call | solution.py:402
  180.6 10.1 %hidden_back.1 = (f32[512,768]{1,0:T(8,128)S(1)}, bf16[512,768]{1,0:T(8,128)(2,1)S(1)}, f32[8,768]{1,0:T(8,128)S(1)}) custom-call(s32[3]{0:T(128)S(1)} %pad_add_fusion.meta, bf16[512,1536]{1,0:T(8,128)(2,1)S(1)} %get-tuple-element.65.du0.right_o, bf16[512,1536]{1,0:T(8,128)(2,1)S(1)} %get-tuple-element.66.du1, bf16[8,48,768]{2,1,0:T(8,128)(2,1)S(1)} %copy-done.5, ...), custom_call_target="tpu_custom_call" | custom-call | flops 3000000000 | bytes 12000000 | tf_op jit(solution)/shard_map/hidden_back/pallas_call | solution.py:443
  195.6 1.5 collective-permute-start.95
  209.0 21.3 %attn_back.1 = (bf16[512,384]{1,0:T(8,128)(2,1)S(1)}, bf16[512,384]{1,0:T(8,128)(2,1)S(1)}, bf16[512,384]{1,0:T(8,128)(2,1)S(1)}, bf16[512,384]{1,0:T(8,128)(2,1...) custom-call(s32[3]{0:T(128)S(1)} %pad_add_fusion.meta, ...), custom_call_target="tpu_custom_call" | custom-call | flops 8000000000 | bytes 20000000 | tf_op jit(solution)/shard_map/attn_back/pallas_call | solution.py:519
  234.8 3.0 collective-permute-start.98
  238.0 2.1 collective-permute-done.98
  242.7 2.0 collective-permute-start.99
  253.8 8.4 %attn_grad.1 = (bf16[8,48,768]{2,1,0:T(8,128)(2,1)S(1)}, bf16[8,48,768]{2,1,0:T(8,128)(2,1)S(1)}, bf16[8,48,768]{2,1,0:T(8,128)(2,1)S(1)}, bf16[8,48,768]{2,1,0:T(8,128)(2,1)}) custom-call(s32[3]{0:T(128)S(1)} %pad_add_fusion.meta, bf16[256,768]{1,0:T(8,128)(2,1)} %get-tuple-element.138.xo, bf16[256,768]{1,0:T(8,128)(2,1)S(1)} %copy-done.55, ...), custom_call_target="tpu_custom_call" | custom-call | flops 3000000000 | bytes 8000000 | tf_op jit(solution)/shard_map/attn_grad/pallas_call | solution.py:615
  264.7 1.5 collective-permute-start.57
  267.6 1.5 collective-permute-start.52
  270.0 2.4 maximum_select_fusion.1
  272.4 2.8 maximum_select_fusion
  275.2 5.3 %collective-permute-done.57 = bf16[8,48,768]{2,1,0:T(8,128)(2,1)} collective-permute-done((bf16[8,48,768]{2,1,0:T(8,128)(2,1)}, bf16[8,48,768]{2,1,0:T(8,128)(2,1)}, u32[]{:S(2)}, u32[]{:S(2)}) %collective-permute-start.57) | collective-permute-done | bytes 589856 | tf_op jit(solution)/shard_map/ppermute | solution.py:646
  283.0 1.5 collective-permute-start.58
  285.2 6.7 %ffn_grad.3 = (bf16[8,48,768]{2,1,0:T(8,128)(2,1)S(1)}, bf16[8,48,768]{2,1,0:T(8,128)(2,1)}, bf16[8,48,768]{2,1,0:T(8,128)(2,1)S(1)}, bf16[8,48,768]{2,1,0:T(8,128)(2,1)}) custom-call(s32[3]{0:T(128)S(1)} %pad_add_fusion.meta, bf16[512,768]{1,0:T(8,128)(2,1)S(1)} %copy-done.42, bf16[512,768]{1,0:T(8,128)(2,1)S(1)} %collective-permute-done.74.left_r, ...), custom_call_target="tpu_custom_call" | custom-call | flops 3000000000 | bytes 8000000 | tf_op jit(solution)/shard_map/ffn_grad/pallas_call | solution.py:574
  291.9 1.6 collective-permute-start.81
  294.1 7.2 %ffn_grad.2 = (bf16[8,48,768]{2,1,0:T(8,128)(2,1)S(1)}, bf16[8,48,768]{2,1,0:T(8,128)(2,1)S(1)}, bf16[8,48,768]{2,1,0:T(8,128)(2,1)S(1)}, bf16[8,48,768]{2,1,0:T(8,128)(2,1)}) custom-call(s32[3]{0:T(128)S(1)} %pad_add_fusion.meta, bf16[512,768]{1,0:T(8,128)(2,1)S(1)} %copy-done.40, bf16[512,768]{1,0:T(8,128)(2,1)S(1)} %collective-permute-done.62.left_r, ...), custom_call_target="tpu_custom_call" | custom-call | flops 3000000000 | bytes 8000000 | tf_op jit(solution)/shard_map/ffn_grad/pallas_call | solution.py:574
  303.8 2.0 collective-permute-start.61
  307.6 2.9 collective-permute-done.60
  310.5 2.1 collective-permute-start.56
  314.1 1.7 collective-permute-done.55
  323.2 1.9 collective-permute-start.77
  325.1 3.9 collective-permute-done.69
  330.1 1.5 collective-permute-start.70
  333.3 1.8 collective-permute-start.65
  335.1 2.0 collective-permute-done.82
  337.9 1.5 collective-permute-start.84
  340.3 2.7 collective-permute-start.79
  344.3 1.9 collective-permute-start.71
  346.2 2.0 collective-permute-done.79
  349.5 1.5 collective-permute-start.73
  352.6 4.6 %collective-permute-done.72 = bf16[48,768]{1,0:T(8,128)(2,1)S(1)} collective-permute-done((bf16[48,768]{1,0:T(8,128)(2,1)S(1)}, bf16[48,768]{1,0:T(8,128)(2,1)S(1)}, u32[]{:S(2)}, u32[]{:S(2)}) %collective-permute-start.72) | collective-permute-done | bytes 73760 | tf_op jit(solution)/shard_map/ppermute | solution.py:646
  359.3 2.5 collective-permute-start.85
  367.4 1.6 multiply_reduce_fusion
  371.0 1.5 collective-permute-start.87
  376.1 1.9 collective-permute-done.89
  380.7 1.7 collective-permute-start.92
  383.9 2.3 collective-permute-done.92
  392.3 1.5 multiply_subtract_fusion
  (461 shorter events, 117.7 us)
Async XLA Ops:
  2.4 12.3 %collective-permute-start.8 = (bf16[48,768]{1,0:T(8,128)(2,1)}, bf16[48,768]{1,0:T(8,128)(2,1)S(1)}, u32[]{:S(2)}, u32[]{:S(2)}) collective-permute-start(bf16[48,768]{1,0:T(8,128)(2,1)} %get-tuple-element.178), channel_id=1, source_target_pairs={{0,8},{2,10},{4,12},{6,14},{8,0},{10,2},{12,4},{14,6},{16,24},{18,... | collective-permute-start | bytes 221192 | tf_op jit(solution)/shard_map/ppermute | solution.py:646
  5.4 9.4 %collective-permute-start.9 = (bf16[48,768]{1,0:T(8,128)(2,1)}, bf16[48,768]{1,0:T(8,128)(2,1)S(1)}, u32[]{:S(2)}, u32[]{:S(2)}) collective-permute-start(bf16[48,768]{1,0:T(8,128)(2,1)} %get-tuple-element.178), channel_id=1, source_target_pairs={{0,16},{2,18},{4,20},{6,22},{8,24},{10,26},{12,28},{14,30},{16,0},... | collective-permute-start | bytes 221192 | tf_op jit(solution)/shard_map/ppermute | solution.py:646
  8.7 12.4 %collective-permute-start.1 = (bf16[48,768]{1,0:T(8,128)(2,1)}, bf16[48,768]{1,0:T(8,128)(2,1)S(1)}, u32[]{:S(2)}, u32[]{:S(2)}) collective-permute-start(bf16[48,768]{1,0:T(8,128)(2,1)} %get-tuple-element.180), channel_id=1, source_target_pairs={{0,8},{2,10},{4,12},{6,14},{8,0},{10,2},{12,4},{14,6},{16,24},{18,... | collective-permute-start | bytes 221192 | tf_op jit(solution)/shard_map/ppermute | solution.py:646
  9.6 12.0 %collective-permute-start.2 = (bf16[48,768]{1,0:T(8,128)(2,1)}, bf16[48,768]{1,0:T(8,128)(2,1)S(1)}, u32[]{:S(2)}, u32[]{:S(2)}) collective-permute-start(bf16[48,768]{1,0:T(8,128)(2,1)} %get-tuple-element.180), channel_id=1, source_target_pairs={{0,16},{2,18},{4,20},{6,22},{8,24},{10,26},{12,28},{14,30},{16,0},... | collective-permute-start | bytes 221192 | tf_op jit(solution)/shard_map/ppermute | solution.py:646
  14.8 10.9 %collective-permute-start.15 = (bf16[48,768]{1,0:T(8,128)(2,1)S(1)}, bf16[48,768]{1,0:T(8,128)(2,1)S(1)}, u32[]{:S(2)}, u32[]{:S(2)}) collective-permute-start(bf16[48,768]{1,0:T(8,128)(2,1)S(1)} %copy-done.102), channel_id=1, source_target_pairs={{0,8},{2,10},{4,12},{6,14},{8,0},{10,2},{12,4},{14,6},{16,24},{18,... | collective-permute-start | bytes 221192 | tf_op jit(solution)/shard_map/ppermute | solution.py:646
  15.4 12.8 %collective-permute-start.16 = (bf16[48,768]{1,0:T(8,128)(2,1)S(1)}, bf16[48,768]{1,0:T(8,128)(2,1)S(1)}, u32[]{:S(2)}, u32[]{:S(2)}) collective-permute-start(bf16[48,768]{1,0:T(8,128)(2,1)S(1)} %copy-done.102), channel_id=1, source_target_pairs={{0,16},{2,18},{4,20},{6,22},{8,24},{10,26},{12,28},{14,30},{16,0},... | collective-permute-start | bytes 221192 | tf_op jit(solution)/shard_map/ppermute | solution.py:646
  21.5 12.5 %collective-permute-start.22 = (bf16[48,768]{1,0:T(8,128)(2,1)S(1)}, bf16[48,768]{1,0:T(8,128)(2,1)S(1)}, u32[]{:S(2)}, u32[]{:S(2)}) collective-permute-start(bf16[48,768]{1,0:T(8,128)(2,1)S(1)} %copy-done.101), channel_id=1, source_target_pairs={{0,8},{2,10},{4,12},{6,14},{8,0},{10,2},{12,4},{14,6},{16,24},{18,... | collective-permute-start | bytes 221192 | tf_op jit(solution)/shard_map/ppermute | solution.py:646
  22.3 12.6 %collective-permute-start.23 = (bf16[48,768]{1,0:T(8,128)(2,1)S(1)}, bf16[48,768]{1,0:T(8,128)(2,1)S(1)}, u32[]{:S(2)}, u32[]{:S(2)}) collective-permute-start(bf16[48,768]{1,0:T(8,128)(2,1)S(1)} %copy-done.101), channel_id=1, source_target_pairs={{0,16},{2,18},{4,20},{6,22},{8,24},{10,26},{12,28},{14,30},{16,0},... | collective-permute-start | bytes 221192 | tf_op jit(solution)/shard_map/ppermute | solution.py:646
  25.8 9.2 %collective-permute-start.24 = (bf16[48,768]{1,0:T(8,128)(2,1)S(1)}, bf16[48,768]{1,0:T(8,128)(2,1)S(1)}, u32[]{:S(2)}, u32[]{:S(2)}) collective-permute-start(bf16[48,768]{1,0:T(8,128)(2,1)S(1)} %copy-done.101), channel_id=1, source_target_pairs={{0,24},{2,26},{4,28},{6,30},{8,16},{10,18},{12,20},{14,22},{16,8},... | collective-permute-start | bytes 221192 | tf_op jit(solution)/shard_map/ppermute | solution.py:646
  28.3 10.4 %collective-permute-start.29 = (bf16[48,768]{1,0:T(8,128)(2,1)S(1)}, bf16[48,768]{1,0:T(8,128)(2,1)S(1)}, u32[]{:S(2)}, u32[]{:S(2)}) collective-permute-start(bf16[48,768]{1,0:T(8,128)(2,1)S(1)} %copy-done.98), channel_id=1, source_target_pairs={{0,8},{2,10},{4,12},{6,14},{8,0},{10,2},{12,4},{14,6},{16,24},{18,... | collective-permute-start | bytes 221192 | tf_op jit(solution)/shard_map/ppermute | solution.py:646
  28.6 11.9 %collective-permute-start.30 = (bf16[48,768]{1,0:T(8,128)(2,1)S(1)}, bf16[48,768]{1,0:T(8,128)(2,1)S(1)}, u32[]{:S(2)}, u32[]{:S(2)}) collective-permute-start(bf16[48,768]{1,0:T(8,128)(2,1)S(1)} %copy-done.98), channel_id=1, source_target_pairs={{0,16},{2,18},{4,20},{6,22},{8,24},{10,26},{12,28},{14,30},{16,0},... | collective-permute-start | bytes 221192 | tf_op jit(solution)/shard_map/ppermute | solution.py:646
  34.9 17.0 %collective-permute-start.36 = (bf16[48,768]{1,0:T(8,128)(2,1)S(1)}, bf16[48,768]{1,0:T(8,128)(2,1)S(1)}, u32[]{:S(2)}, u32[]{:S(2)}) collective-permute-start(bf16[48,768]{1,0:T(8,128)(2,1)S(1)} %copy-done.97), channel_id=1, source_target_pairs={{0,8},{2,10},{4,12},{6,14},{8,0},{10,2},{12,4},{14,6},{16,24},{18,... | collective-permute-start | bytes 221192 | tf_op jit(solution)/shard_map/ppermute | solution.py:646
  35.0 18.6 %collective-permute-start.37 = (bf16[48,768]{1,0:T(8,128)(2,1)S(1)}, bf16[48,768]{1,0:T(8,128)(2,1)S(1)}, u32[]{:S(2)}, u32[]{:S(2)}) collective-permute-start(bf16[48,768]{1,0:T(8,128)(2,1)S(1)} %copy-done.97), channel_id=1, source_target_pairs={{0,16},{2,18},{4,20},{6,22},{8,24},{10,26},{12,28},{14,30},{16,0},... | collective-permute-start | bytes 221192 | tf_op jit(solution)/shard_map/ppermute | solution.py:646
  40.5 9.9 %collective-permute-start.4 = (bf16[4,48,768]{2,1,0:T(8,128)(2,1)S(1)}, bf16[4,48,768]{2,1,0:T(8,128)(2,1)S(1)}, u32[]{:S(2)}, u32[]{:S(2)}) collective-permute-start(bf16[4,48,768]{2,1,0:T(8,128)(2,1)S(1)} %pad_maximum_fusion), channel_id=1, source_target_pairs={{0,4},{2,6},{4,0},{6,2},{8,12},{10,14},{12,8},{14,10},{16,20},{18,... | collective-permute-start | bytes 884744 | tf_op jit(solution)/shard_map/ppermute | solution.py:646
  42.1 14.7 %collective-permute-start.18 = (bf16[4,48,768]{2,1,0:T(8,128)(2,1)S(1)}, bf16[4,48,768]{2,1,0:T(8,128)(2,1)S(1)}, u32[]{:S(2)}, u32[]{:S(2)}) collective-permute-start(bf16[4,48,768]{2,1,0:T(8,128)(2,1)S(1)} %pad_maximum_fusion.2), channel_id=1, source_target_pairs={{0,4},{2,6},{4,0},{6,2},{8,12},{10,14},{12,8},{14,10},{16,20},{18,... | collective-permute-start | bytes 884744 | tf_op jit(solution)/shard_map/ppermute | solution.py:646
  45.5 8.6 %collective-permute-start.38 = (bf16[48,768]{1,0:T(8,128)(2,1)S(1)}, bf16[48,768]{1,0:T(8,128)(2,1)S(1)}, u32[]{:S(2)}, u32[]{:S(2)}) collective-permute-start(bf16[48,768]{1,0:T(8,128)(2,1)S(1)} %copy-done.97), channel_id=1, source_target_pairs={{0,24},{2,26},{4,28},{6,30},{8,16},{10,18},{12,20},{14,22},{16,8},... | collective-permute-start | bytes 221192 | tf_op jit(solution)/shard_map/ppermute | solution.py:646
  52.0 11.1 %collective-permute-start.32 = (bf16[4,48,768]{2,1,0:T(8,128)(2,1)S(1)}, bf16[4,48,768]{2,1,0:T(8,128)(2,1)S(1)}, u32[]{:S(2)}, u32[]{:S(2)}) collective-permute-start(bf16[4,48,768]{2,1,0:T(8,128)(2,1)S(1)} %pad_maximum_fusion.4), channel_id=1, source_target_pairs={{0,4},{2,6},{4,0},{6,2},{8,12},{10,14},{12,8},{14,10},{16,20},{18,... | collective-permute-start | bytes 884744 | tf_op jit(solution)/shard_map/ppermute | solution.py:646
  53.5 24.9 %collective-permute-start.12 = (bf16[8,48,768]{2,1,0:T(8,128)(2,1)S(1)}, bf16[8,48,768]{2,1,0:T(8,128)(2,1)}, u32[]{:S(2)}, u32[]{:S(2)}) collective-permute-start(bf16[8,48,768]{2,1,0:T(8,128)(2,1)S(1)} %constant_dynamic-update-slice_fusion.5.refs_4_), channel_id=1, source_target_pairs={{0,4},{2,6},{4,0},{6,2},{8,12},{10,14},{12,8},{14,10},{16,20},{18,... | collective-permute-start | bytes 1769480 | tf_op jit(solution)/shard_map/ppermute | solution.py:646
  54.1 26.1 %collective-permute-start.13 = (bf16[8,48,768]{2,1,0:T(8,128)(2,1)S(1)}, bf16[8,48,768]{2,1,0:T(8,128)(2,1)S(1)}, u32[]{:S(2)}, u32[]{:S(2)}) collective-permute-start(bf16[8,48,768]{2,1,0:T(8,128)(2,1)S(1)} %constant_dynamic-update-slice_fusion.5.refs_4_), channel_id=1, source_target_pairs={{0,1},{1,0},{2,3},{3,2},{4,5},{5,4},{6,7},{7,6},{8,9},{9,8},{10,11... | collective-permute-start | bytes 1769480 | tf_op jit(solution)/shard_map/ppermute | solution.py:642
  56.8 21.9 %collective-permute-start.5 = (bf16[8,48,768]{2,1,0:T(8,128)(2,1)S(1)}, bf16[8,48,768]{2,1,0:T(8,128)(2,1)}, u32[]{:S(2)}, u32[]{:S(2)}) collective-permute-start(bf16[8,48,768]{2,1,0:T(8,128)(2,1)S(1)} %constant_dynamic-update-slice_fusion.refs_0_), channel_id=1, source_target_pairs={{0,2},{2,0},{4,6},{6,4},{8,10},{10,8},{12,14},{14,12},{16,18},{18,... | collective-permute-start | bytes 1769480 | tf_op jit(solution)/shard_map/ppermute | solution.py:646
  58.3 17.9 %collective-permute-start = (bf16[256,768]{1,0:T(8,128)(2,1)S(1)}, bf16[256,768]{1,0:T(8,128)(2,1)S(1)}, u32[]{:S(2)}, u32[]{:S(2)}) collective-permute-start(bf16[256,768]{1,0:T(8,128)(2,1)S(1)} %get-tuple-element.137.zr), channel_id=1, source_target_pairs={{0,1},{1,0},{2,3},{3,2},{4,5},{5,4},{6,7},{7,6},{8,9},{9,8},{10,11... | collective-permute-start | bytes 1179656 | tf_op jit(solution)/shard_map/ppermute | solution.py:642
  63.1 13.0 %collective-permute-start.39 = (bf16[4,48,768]{2,1,0:T(8,128)(2,1)S(1)}, bf16[4,48,768]{2,1,0:T(8,128)(2,1)S(1)}, u32[]{:S(2)}, u32[]{:S(2)}) collective-permute-start(bf16[4,48,768]{2,1,0:T(8,128)(2,1)S(1)} %pad_maximum_fusion.5), channel_id=1, source_target_pairs={{0,2},{2,0},{4,6},{6,4},{8,10},{10,8},{12,14},{14,12},{16,18},{18,... | collective-permute-start | bytes 884744 | tf_op jit(solution)/shard_map/ppermute | solution.py:646
  77.0 16.1 %collective-permute-start.19 = (bf16[8,48,768]{2,1,0:T(8,128)(2,1)S(1)}, bf16[8,48,768]{2,1,0:T(8,128)(2,1)S(1)}, u32[]{:S(2)}, u32[]{:S(2)}) collective-permute-start(bf16[8,48,768]{2,1,0:T(8,128)(2,1)S(1)} %constant_dynamic-update-slice_fusion.10.refs_0_), channel_id=1, source_target_pairs={{0,2},{2,0},{4,6},{6,4},{8,10},{10,8},{12,14},{14,12},{16,18},{18,... | collective-permute-start | bytes 1769480 | tf_op jit(solution)/shard_map/ppermute | solution.py:646
  78.4 16.2 %collective-permute-start.20 = (bf16[8,48,768]{2,1,0:T(8,128)(2,1)S(1)}, bf16[8,48,768]{2,1,0:T(8,128)(2,1)S(1)}, u32[]{:S(2)}, u32[]{:S(2)}) collective-permute-start(bf16[8,48,768]{2,1,0:T(8,128)(2,1)S(1)} %constant_dynamic-update-slice_fusion.10.refs_0_), channel_id=1, source_target_pairs={{0,1},{1,0},{2,3},{3,2},{4,5},{5,4},{6,7},{7,6},{8,9},{9,8},{10,11... | collective-permute-start | bytes 1769480 | tf_op jit(solution)/shard_map/ppermute | solution.py:642
  78.7 15.9 %collective-permute-start.26 = (bf16[8,48,768]{2,1,0:T(8,128)(2,1)S(1)}, bf16[8,48,768]{2,1,0:T(8,128)(2,1)S(1)}, u32[]{:S(2)}, u32[]{:S(2)}) collective-permute-start(bf16[8,48,768]{2,1,0:T(8,128)(2,1)S(1)} %constant_dynamic-update-slice_fusion.15.refs_4_), channel_id=1, source_target_pairs={{0,4},{2,6},{4,0},{6,2},{8,12},{10,14},{12,8},{14,10},{16,20},{18,... | collective-permute-start | bytes 1769480 | tf_op jit(solution)/shard_map/ppermute | solution.py:646
  80.2 14.9 %collective-permute-start.27 = (bf16[8,48,768]{2,1,0:T(8,128)(2,1)S(1)}, bf16[8,48,768]{2,1,0:T(8,128)(2,1)S(1)}, u32[]{:S(2)}, u32[]{:S(2)}) collective-permute-start(bf16[8,48,768]{2,1,0:T(8,128)(2,1)S(1)} %constant_dynamic-update-slice_fusion.15.refs_4_), channel_id=1, source_target_pairs={{0,1},{1,0},{2,3},{3,2},{4,5},{5,4},{6,7},{7,6},{8,9},{9,8},{10,11... | collective-permute-start | bytes 1769480 | tf_op jit(solution)/shard_map/ppermute | solution.py:642
  83.1 22.4 %collective-permute-start.33 = (bf16[8,48,768]{2,1,0:T(8,128)(2,1)}, bf16[8,48,768]{2,1,0:T(8,128)(2,1)}, u32[]{:S(2)}, u32[]{:S(2)}) collective-permute-start(bf16[8,48,768]{2,1,0:T(8,128)(2,1)} %constant_dynamic-update-slice_fusion.20.refs_0_), channel_id=1, source_target_pairs={{0,2},{2,0},{4,6},{6,4},{8,10},{10,8},{12,14},{14,12},{16,18},{18,... | collective-permute-start | bytes 1769480 | tf_op jit(solution)/shard_map/ppermute | solution.py:646
  93.1 16.6 %collective-permute-start.40 = (bf16[8,48,768]{2,1,0:T(8,128)(2,1)}, bf16[8,48,768]{2,1,0:T(8,128)(2,1)}, u32[]{:S(2)}, u32[]{:S(2)}) collective-permute-start(bf16[8,48,768]{2,1,0:T(8,128)(2,1)} %constant_dynamic-update-slice_fusion.25.refs_4_), channel_id=1, source_target_pairs={{0,4},{2,6},{4,0},{6,2},{8,12},{10,14},{12,8},{14,10},{16,20},{18,... | collective-permute-start | bytes 1769480 | tf_op jit(solution)/shard_map/ppermute | solution.py:646
  94.6 15.6 %collective-permute-start.14 = (bf16[8,48,768]{2,1,0:T(8,128)(2,1)}, bf16[8,48,768]{2,1,0:T(8,128)(2,1)}, u32[]{:S(2)}, u32[]{:S(2)}) collective-permute-start(bf16[8,48,768]{2,1,0:T(8,128)(2,1)} %collective-permute-done.12.refs_5_), channel_id=1, source_target_pairs={{0,1},{1,0},{2,3},{3,2},{4,5},{5,4},{6,7},{7,6},{8,9},{9,8},{10,11... | collective-permute-start | bytes 1769480 | tf_op jit(solution)/shard_map/ppermute | solution.py:642
  94.6 15.6 %collective-permute-start.7 = (bf16[8,48,768]{2,1,0:T(8,128)(2,1)}, bf16[8,48,768]{2,1,0:T(8,128)(2,1)}, u32[]{:S(2)}, u32[]{:S(2)}) collective-permute-start(bf16[8,48,768]{2,1,0:T(8,128)(2,1)} %collective-permute-done.5.refs_1_), channel_id=1, source_target_pairs={{0,1},{1,0},{2,3},{3,2},{4,5},{5,4},{6,7},{7,6},{8,9},{9,8},{10,11... | collective-permute-start | bytes 1769480 | tf_op jit(solution)/shard_map/ppermute | solution.py:642
  95.1 15.6 %collective-permute-start.21 = (bf16[8,48,768]{2,1,0:T(8,128)(2,1)S(1)}, bf16[8,48,768]{2,1,0:T(8,128)(2,1)}, u32[]{:S(2)}, u32[]{:S(2)}) collective-permute-start(bf16[8,48,768]{2,1,0:T(8,128)(2,1)S(1)} %collective-permute-done.19.refs_1_), channel_id=1, source_target_pairs={{0,1},{1,0},{2,3},{3,2},{4,5},{5,4},{6,7},{7,6},{8,9},{9,8},{10,11... | collective-permute-start | bytes 1769480 | tf_op jit(solution)/shard_map/ppermute | solution.py:642
  105.5 32.3 %collective-permute-start.28 = (bf16[8,48,768]{2,1,0:T(8,128)(2,1)S(1)}, bf16[8,48,768]{2,1,0:T(8,128)(2,1)}, u32[]{:S(2)}, u32[]{:S(2)}) collective-permute-start(bf16[8,48,768]{2,1,0:T(8,128)(2,1)S(1)} %collective-permute-done.26.refs_5_), channel_id=1, source_target_pairs={{0,1},{1,0},{2,3},{3,2},{4,5},{5,4},{6,7},{7,6},{8,9},{9,8},{10,11... | collective-permute-start | bytes 1769480 | tf_op jit(solution)/shard_map/ppermute | solution.py:642
  109.7 46.8 %collective-permute-start.34 = (bf16[8,48,768]{2,1,0:T(8,128)(2,1)}, bf16[8,48,768]{2,1,0:T(8,128)(2,1)S(1)}, u32[]{:S(2)}, u32[]{:S(2)}) collective-permute-start(bf16[8,48,768]{2,1,0:T(8,128)(2,1)} %constant_dynamic-update-slice_fusion.20.refs_0_), channel_id=1, source_target_pairs={{0,1},{1,0},{2,3},{3,2},{4,5},{5,4},{6,7},{7,6},{8,9},{9,8},{10,11... | collective-permute-start | bytes 1769480 | tf_op jit(solution)/shard_map/ppermute | solution.py:642
  110.2 46.3 %collective-permute-start.41 = (bf16[8,48,768]{2,1,0:T(8,128)(2,1)}, bf16[8,48,768]{2,1,0:T(8,128)(2,1)S(1)}, u32[]{:S(2)}, u32[]{:S(2)}) collective-permute-start(bf16[8,48,768]{2,1,0:T(8,128)(2,1)} %constant_dynamic-update-slice_fusion.25.refs_4_), channel_id=1, source_target_pairs={{0,1},{1,0},{2,3},{3,2},{4,5},{5,4},{6,7},{7,6},{8,9},{9,8},{10,11... | collective-permute-start | bytes 1769480 | tf_op jit(solution)/shard_map/ppermute | solution.py:642
  110.3 46.3 %collective-permute-start.35 = (bf16[8,48,768]{2,1,0:T(8,128)(2,1)}, bf16[8,48,768]{2,1,0:T(8,128)(2,1)S(1)}, u32[]{:S(2)}, u32[]{:S(2)}) collective-permute-start(bf16[8,48,768]{2,1,0:T(8,128)(2,1)} %collective-permute-done.33.refs_1_), channel_id=1, source_target_pairs={{0,1},{1,0},{2,3},{3,2},{4,5},{5,4},{6,7},{7,6},{8,9},{9,8},{10,11... | collective-permute-start | bytes 1769480 | tf_op jit(solution)/shard_map/ppermute | solution.py:642
  110.7 45.8 %collective-permute-start.42 = (bf16[8,48,768]{2,1,0:T(8,128)(2,1)}, bf16[8,48,768]{2,1,0:T(8,128)(2,1)S(1)}, u32[]{:S(2)}, u32[]{:S(2)}) collective-permute-start(bf16[8,48,768]{2,1,0:T(8,128)(2,1)} %collective-permute-done.40.refs_5_), channel_id=1, source_target_pairs={{0,1},{1,0},{2,3},{3,2},{4,5},{5,4},{6,7},{7,6},{8,9},{9,8},{10,11... | collective-permute-start | bytes 1769480 | tf_op jit(solution)/shard_map/ppermute | solution.py:642
  137.8 18.7 %collective-permute-start.43 = (bf16[256,768]{1,0:T(8,128)(2,1)S(1)}, bf16[256,768]{1,0:T(8,128)(2,1)S(1)}, u32[]{:S(2)}, u32[]{:S(2)}) collective-permute-start(bf16[256,768]{1,0:T(8,128)(2,1)S(1)} %copy-done.88), channel_id=1, source_target_pairs={{0,1},{1,0},{2,3},{3,2},{4,5},{5,4},{6,7},{7,6},{8,9},{9,8},{10,11... | collective-permute-start | bytes 1179656 | tf_op jit(solution)/shard_map/ppermute | solution.py:642
  193.0 41.1 %collective-permute-start.46 = (bf16[256,768]{1,0:T(8,128)(2,1)}, bf16[256,768]{1,0:T(8,128)(2,1)S(1)}, u32[]{:S(2)}, u32[]{:S(2)}) collective-permute-start(bf16[256,768]{1,0:T(8,128)(2,1)} %get-tuple-element.138.xo), channel_id=1, source_target_pairs={{0,1},{1,0},{2,3},{3,2},{4,5},{5,4},{6,7},{7,6},{8,9},{9,8},{10,11... | collective-permute-start | bytes 1179656 | tf_op jit(solution)/shard_map/ppermute | solution.py:642
  193.4 49.2 %collective-permute-start.47 = (bf16[512,768]{1,0:T(8,128)(2,1)}, bf16[512,768]{1,0:T(8,128)(2,1)}, u32[]{:S(2)}, u32[]{:S(2)}) collective-permute-start(bf16[512,768]{1,0:T(8,128)(2,1)} %copy-done.43), channel_id=1, source_target_pairs={{0,1},{1,0},{2,3},{3,2},{4,5},{5,4},{6,7},{7,6},{8,9},{9,8},{10,11... | collective-permute-start | bytes 2359304 | tf_op jit(solution)/shard_map/ppermute | solution.py:642
  194.1 39.3 %collective-permute-start.94 = (f32[7680]{0:T(1024)S(1)}, f32[7680]{0:T(1024)S(1)}, u32[]{:S(2)}, u32[]{:S(2)}) collective-permute-start(f32[7680]{0:T(1024)S(1)} %add.389), channel_id=1, source_target_pairs={{0,2},{2,0},{4,6},{6,4},{8,10},{10,8},{12,14},{14,12},{16,18},{18,... | collective-permute-start | bytes 92168 | tf_op jit(solution)/shard_map/ppermute | solution.py:646
  195.6 37.9 %collective-permute-start.95 = (f32[7680]{0:T(1024)S(1)}, f32[7680]{0:T(1024)S(1)}, u32[]{:S(2)}, u32[]{:S(2)}) collective-permute-start(f32[7680]{0:T(1024)S(1)} %add.389), channel_id=1, source_target_pairs={{0,4},{2,6},{4,0},{6,2},{8,12},{10,14},{12,8},{14,10},{16,20},{18,... | collective-permute-start | bytes 92168 | tf_op jit(solution)/shard_map/ppermute | solution.py:646
  197.1 36.9 %collective-permute-start.96 = (f32[7680]{0:T(1024)S(1)}, f32[7680]{0:T(1024)S(1)}, u32[]{:S(2)}, u32[]{:S(2)}) collective-permute-start(f32[7680]{0:T(1024)S(1)} %add.389), channel_id=1, source_target_pairs={{0,6},{2,4},{4,2},{6,0},{8,14},{10,12},{12,10},{14,8},{16,22},{18,... | collective-permute-start | bytes 92168 | tf_op jit(solution)/shard_map/ppermute | solution.py:646
  240.8 29.1 %collective-permute-start.45 = (f32[256,768]{1,0:T(8,128)}, f32[256,768]{1,0:T(8,128)}, u32[]{:S(2)}, u32[]{:S(2)}) collective-permute-start(f32[256,768]{1,0:T(8,128)} %get-tuple-element.77), channel_id=1, source_target_pairs={{0,1},{1,0},{2,3},{3,2},{4,5},{5,4},{6,7},{7,6},{8,9},{9,8},{10,11... | collective-permute-start | bytes 2359304 | tf_op jit(solution)/shard_map/ppermute | solution.py:642
  242.1 43.1 %collective-permute-start.75 = (bf16[512,1536]{1,0:T(8,128)(2,1)}, bf16[512,1536]{1,0:T(8,128)(2,1)}, u32[]{:S(2)}, u32[]{:S(2)}) collective-permute-start(bf16[512,1536]{1,0:T(8,128)(2,1)} %get-tuple-element.59.f1), channel_id=1, source_target_pairs={{0,1},{1,0},{2,3},{3,2},{4,5},{5,4},{6,7},{7,6},{8,9},{9,8},{10,11... | collective-permute-start | bytes 4718600 | tf_op jit(solution)/shard_map/ppermute | solution.py:642
  242.1 51.9 %collective-permute-start.63 = (bf16[512,1536]{1,0:T(8,128)(2,1)S(1)}, bf16[512,1536]{1,0:T(8,128)(2,1)}, u32[]{:S(2)}, u32[]{:S(2)}) collective-permute-start(bf16[512,1536]{1,0:T(8,128)(2,1)S(1)} %get-tuple-element.66.du1), channel_id=1, source_target_pairs={{0,1},{1,0},{2,3},{3,2},{4,5},{5,4},{6,7},{7,6},{8,9},{9,8},{10,11... | collective-permute-start | bytes 4718600 | tf_op jit(solution)/shard_map/ppermute | solution.py:642
  242.6 25.0 %collective-permute-start.44 = (bf16[256,768]{1,0:T(8,128)(2,1)}, bf16[256,768]{1,0:T(8,128)(2,1)}, u32[]{:S(2)}, u32[]{:S(2)}) collective-permute-start(bf16[256,768]{1,0:T(8,128)(2,1)} %copy-done.56), channel_id=1, source_target_pairs={{0,1},{1,0},{2,3},{3,2},{4,5},{5,4},{6,7},{7,6},{8,9},{9,8},{10,11... | collective-permute-start | bytes 1179656 | tf_op jit(solution)/shard_map/ppermute | solution.py:642
  242.7 22.0 %collective-permute-start.99 = (f32[7680]{0:T(1024)}, f32[7680]{0:T(1024)}, u32[]{:S(2)}, u32[]{:S(2)}) collective-permute-start(f32[7680]{0:T(1024)} %copy-done.96), channel_id=1, source_target_pairs={{0,24},{2,26},{4,28},{6,30},{8,16},{10,18},{12,20},{14,22},{16,8},... | collective-permute-start | bytes 92168 | tf_op jit(solution)/shard_map/ppermute | solution.py:646
  264.7 15.7 %collective-permute-start.57 = (bf16[8,48,768]{2,1,0:T(8,128)(2,1)}, bf16[8,48,768]{2,1,0:T(8,128)(2,1)}, u32[]{:S(2)}, u32[]{:S(2)}) collective-permute-start(bf16[8,48,768]{2,1,0:T(8,128)(2,1)} %get-tuple-element.90), channel_id=1, source_target_pairs={{0,4},{2,6},{4,0},{6,2},{8,12},{10,14},{12,8},{14,10},{16,20},{18,... | collective-permute-start | bytes 1769480 | tf_op jit(solution)/shard_map/ppermute | solution.py:646
  267.6 15.4 %collective-permute-start.52 = (bf16[8,48,768]{2,1,0:T(8,128)(2,1)}, bf16[8,48,768]{2,1,0:T(8,128)(2,1)S(1)}, u32[]{:S(2)}, u32[]{:S(2)}) collective-permute-start(bf16[8,48,768]{2,1,0:T(8,128)(2,1)} %copy-done.52), channel_id=1, source_target_pairs={{0,2},{2,0},{4,6},{6,4},{8,10},{10,8},{12,14},{14,12},{16,18},{18,... | collective-permute-start | bytes 1769480 | tf_op jit(solution)/shard_map/ppermute | solution.py:646
  270.0 14.6 %collective-permute-start.74 = (bf16[512,768]{1,0:T(8,128)(2,1)}, bf16[512,768]{1,0:T(8,128)(2,1)S(1)}, u32[]{:S(2)}, u32[]{:S(2)}) collective-permute-start(bf16[512,768]{1,0:T(8,128)(2,1)} %copy-done.41), channel_id=1, source_target_pairs={{0,1},{1,0},{2,3},{3,2},{4,5},{5,4},{6,7},{7,6},{8,9},{9,8},{10,11... | collective-permute-start | bytes 2359304 | tf_op jit(solution)/shard_map/ppermute | solution.py:642
  280.4 13.0 %collective-permute-start.62 = (bf16[512,768]{1,0:T(8,128)(2,1)S(1)}, bf16[512,768]{1,0:T(8,128)(2,1)S(1)}, u32[]{:S(2)}, u32[]{:S(2)}) collective-permute-start(bf16[512,768]{1,0:T(8,128)(2,1)S(1)} %copy-done.40), channel_id=1, source_target_pairs={{0,1},{1,0},{2,3},{3,2},{4,5},{5,4},{6,7},{7,6},{8,9},{9,8},{10,11... | collective-permute-start | bytes 2359304 | tf_op jit(solution)/shard_map/ppermute | solution.py:642
  283.0 18.3 %collective-permute-start.58 = (bf16[4,48,768]{2,1,0:T(8,128)(2,1)S(1)}, bf16[4,48,768]{2,1,0:T(8,128)(2,1)S(1)}, u32[]{:S(2)}, u32[]{:S(2)}) collective-permute-start(bf16[4,48,768]{2,1,0:T(8,128)(2,1)S(1)} %get-tuple-element.132), channel_id=1, source_target_pairs={{0,2},{2,0},{4,6},{6,4},{8,10},{10,8},{12,14},{14,12},{16,18},{18,... | collective-permute-start | bytes 884744 | tf_op jit(solution)/shard_map/ppermute | solution.py:646
  284.6 19.2 %collective-permute-start.53 = (bf16[4,48,768]{2,1,0:T(8,128)(2,1)S(1)}, bf16[4,48,768]{2,1,0:T(8,128)(2,1)S(1)}, u32[]{:S(2)}, u32[]{:S(2)}) collective-permute-start(bf16[4,48,768]{2,1,0:T(8,128)(2,1)S(1)} %get-tuple-element.134), channel_id=1, source_target_pairs={{0,4},{2,6},{4,0},{6,2},{8,12},{10,14},{12,8},{14,10},{16,20},{18,... | collective-permute-start | bytes 884744 | tf_op jit(solution)/shard_map/ppermute | solution.py:646
  291.9 27.9 %collective-permute-start.81 = (bf16[8,48,768]{2,1,0:T(8,128)(2,1)}, bf16[8,48,768]{2,1,0:T(8,128)(2,1)}, u32[]{:S(2)}, u32[]{:S(2)}) collective-permute-start(bf16[8,48,768]{2,1,0:T(8,128)(2,1)} %get-tuple-element.98), channel_id=1, source_target_pairs={{0,4},{2,6},{4,0},{6,2},{8,12},{10,14},{12,8},{14,10},{16,20},{18,... | collective-permute-start | bytes 1769480 | tf_op jit(solution)/shard_map/ppermute | solution.py:646
  293.5 28.5 %collective-permute-start.76 = (bf16[8,48,768]{2,1,0:T(8,128)(2,1)}, bf16[8,48,768]{2,1,0:T(8,128)(2,1)}, u32[]{:S(2)}, u32[]{:S(2)}) collective-permute-start(bf16[8,48,768]{2,1,0:T(8,128)(2,1)} %get-tuple-element.96), channel_id=1, source_target_pairs={{0,2},{2,0},{4,6},{6,4},{8,10},{10,8},{12,14},{14,12},{16,18},{18,... | collective-permute-start | bytes 1769480 | tf_op jit(solution)/shard_map/ppermute | solution.py:646
  313.3 15.6 %collective-permute-start.69 = (bf16[8,48,768]{2,1,0:T(8,128)(2,1)}, bf16[8,48,768]{2,1,0:T(8,128)(2,1)}, u32[]{:S(2)}, u32[]{:S(2)}) collective-permute-start(bf16[8,48,768]{2,1,0:T(8,128)(2,1)} %get-tuple-element.94), channel_id=1, source_target_pairs={{0,4},{2,6},{4,0},{6,2},{8,12},{10,14},{12,8},{14,10},{16,20},{18,... | collective-permute-start | bytes 1769480 | tf_op jit(solution)/shard_map/ppermute | solution.py:646
  315.7 16.4 %collective-permute-start.64 = (bf16[8,48,768]{2,1,0:T(8,128)(2,1)S(1)}, bf16[8,48,768]{2,1,0:T(8,128)(2,1)}, u32[]{:S(2)}, u32[]{:S(2)}) collective-permute-start(bf16[8,48,768]{2,1,0:T(8,128)(2,1)S(1)} %get-tuple-element.92), channel_id=1, source_target_pairs={{0,2},{2,0},{4,6},{6,4},{8,10},{10,8},{12,14},{14,12},{16,18},{18,... | collective-permute-start | bytes 1769480 | tf_op jit(solution)/shard_map/ppermute | solution.py:646
  321.0 16.1 %collective-permute-start.82 = (bf16[4,48,768]{2,1,0:T(8,128)(2,1)S(1)}, bf16[4,48,768]{2,1,0:T(8,128)(2,1)S(1)}, u32[]{:S(2)}, u32[]{:S(2)}) collective-permute-start(bf16[4,48,768]{2,1,0:T(8,128)(2,1)S(1)} %get-tuple-element.124), channel_id=1, source_target_pairs={{0,2},{2,0},{4,6},{6,4},{8,10},{10,8},{12,14},{14,12},{16,18},{18,... | collective-permute-start | bytes 884744 | tf_op jit(solution)/shard_map/ppermute | solution.py:646
  323.2 16.2 %collective-permute-start.77 = (bf16[4,48,768]{2,1,0:T(8,128)(2,1)S(1)}, bf16[4,48,768]{2,1,0:T(8,128)(2,1)S(1)}, u32[]{:S(2)}, u32[]{:S(2)}) collective-permute-start(bf16[4,48,768]{2,1,0:T(8,128)(2,1)S(1)} %get-tuple-element.126), channel_id=1, source_target_pairs={{0,4},{2,6},{4,0},{6,2},{8,12},{10,14},{12,8},{14,10},{16,20},{18,... | collective-permute-start | bytes 884744 | tf_op jit(solution)/shard_map/ppermute | solution.py:646
  330.1 10.2 %collective-permute-start.70 = (bf16[4,48,768]{2,1,0:T(8,128)(2,1)S(1)}, bf16[4,48,768]{2,1,0:T(8,128)(2,1)S(1)}, u32[]{:S(2)}, u32[]{:S(2)}) collective-permute-start(bf16[4,48,768]{2,1,0:T(8,128)(2,1)S(1)} %get-tuple-element.128), channel_id=1, source_target_pairs={{0,2},{2,0},{4,6},{6,4},{8,10},{10,8},{12,14},{14,12},{16,18},{18,... | collective-permute-start | bytes 884744 | tf_op jit(solution)/shard_map/ppermute | solution.py:646
  333.3 9.8 %collective-permute-start.65 = (bf16[4,48,768]{2,1,0:T(8,128)(2,1)S(1)}, bf16[4,48,768]{2,1,0:T(8,128)(2,1)S(1)}, u32[]{:S(2)}, u32[]{:S(2)}) collective-permute-start(bf16[4,48,768]{2,1,0:T(8,128)(2,1)S(1)} %get-tuple-element.130), channel_id=1, source_target_pairs={{0,4},{2,6},{4,0},{6,2},{8,12},{10,14},{12,8},{14,10},{16,20},{18,... | collective-permute-start | bytes 884744 | tf_op jit(solution)/shard_map/ppermute | solution.py:646
  337.9 28.2 %collective-permute-start.83 = (bf16[48,768]{1,0:T(8,128)(2,1)}, bf16[48,768]{1,0:T(8,128)(2,1)S(1)}, u32[]{:S(2)}, u32[]{:S(2)}) collective-permute-start(bf16[48,768]{1,0:T(8,128)(2,1)} %get-tuple-element.139), channel_id=1, source_target_pairs={{0,8},{2,10},{4,12},{6,14},{8,0},{10,2},{12,4},{14,6},{16,24},{18,... | collective-permute-start | bytes 221192 | tf_op jit(solution)/shard_map/ppermute | solution.py:646
  337.9 28.2 %collective-permute-start.84 = (bf16[48,768]{1,0:T(8,128)(2,1)}, bf16[48,768]{1,0:T(8,128)(2,1)S(1)}, u32[]{:S(2)}, u32[]{:S(2)}) collective-permute-start(bf16[48,768]{1,0:T(8,128)(2,1)} %get-tuple-element.141), channel_id=1, source_target_pairs={{0,16},{2,18},{4,20},{6,22},{8,24},{10,26},{12,28},{14,30},{16,0},... | collective-permute-start | bytes 221192 | tf_op jit(solution)/shard_map/ppermute | solution.py:646
  348.2 9.0 %collective-permute-start.72 = (bf16[48,768]{1,0:T(8,128)(2,1)S(1)}, bf16[48,768]{1,0:T(8,128)(2,1)S(1)}, u32[]{:S(2)}, u32[]{:S(2)}) collective-permute-start(bf16[48,768]{1,0:T(8,128)(2,1)S(1)} %get-tuple-element.147), channel_id=1, source_target_pairs={{0,16},{2,18},{4,20},{6,22},{8,24},{10,26},{12,28},{14,30},{16,0},... | collective-permute-start | bytes 221192 | tf_op jit(solution)/shard_map/ppermute | solution.py:646
  (146 other events, 1447.2 us)
